TPU v7x, 128 devices: a whole 4x4x4 slice. The times are simulated.
128 devices in a mesh: dp: 16 (over z, y_hi, core), ctx: 8 (over y_lo, x).
Axes of the slice: x: 4, y: 4 (y_hi: 2, y_lo: 2; y = y_hi * 2 + y_lo), z: 4, core: 2. Of those that a mesh axis runs over, the one named last changes fastest.
Arguments:
- residual_in: bfloat16 [16, 1024, 1536], P('dp', 'ctx'), may hold values from -64 to 64
- query_rows: bfloat16 [16, 1024, 1536], P('dp', 'ctx'), may hold values from -6 to 6
- key_rows: bfloat16 [16, 1024, 1536], P('dp', 'ctx'), may hold values from -6 to 6
- value_rows: bfloat16 [16, 1024, 1536], P('dp', 'ctx'), may hold values from -6 to 6
- lengths: int32 [16], P('dp'), may hold values from 256 to 1024, as said below
- out_weight: bfloat16 [1536, 1536], replicated, may hold values from -0.15625 to 0.15625
- norm_gain: float32 [1536], replicated, may hold values from 0.25 to 1.75
- conv_kernel: float32 [31, 1536], replicated, may hold values from -1 to 1
- conv_bias: float32 [1536], replicated, may hold values from -3 to 3
- conv_gain: float32 [1536], replicated, may hold values from 0.25 to 1.75
- point_weight: bfloat16 [1536, 1536], replicated, may hold values from -0.15625 to 0.15625
- grad_out: bfloat16 [16, 1024, 1536], P('dp', 'ctx'), may hold values from -6 to 6
Outputs:
- block_out: bfloat16 [16, 1024, 1536], P('dp', 'ctx')
- grad_residual: bfloat16 [16, 1024, 1536], P('dp', 'ctx')
- grad_query: bfloat16 [16, 1024, 1536], P('dp', 'ctx')
- grad_key: bfloat16 [16, 1024, 1536], P('dp', 'ctx')
- grad_value: bfloat16 [16, 1024, 1536], P('dp', 'ctx')
- grad_out_weight: float32 [1536, 1536], P(None, ('dp', 'ctx'))
- grad_point_weight: float32 [1536, 1536], P(None, ('dp', 'ctx'))
- grad_kernel: float32 [31, 1536], P(None, ('dp', 'ctx'))
- grad_vectors: float32 [3, 1536], P(None, ('dp', 'ctx'))
Inputs may be any that keep to these rules, and one draw needn't show every extreme that they name: `lengths`: in every draw some utterance has all 1024 frames.
All inputs are finite; a program needn't handle non-finite values.
Results may differ from a plain program's by a relative error of at most 0.028.
Values may be sent and summed in bfloat16 or wider, within the bound.
A program may use at most 192 MiB of HBM per device.

v0:
```python
import jax
import jax.numpy as jnp
from jax import lax
from jax.sharding import PartitionSpec as P

HEADS = 24
HEAD_DIM = 64


NEG_FILL = -1e30
EPSILON = 1e-05


def passed_along(shard, axis, by):
    peers = lax.axis_size(axis)
    return lax.ppermute(shard, axis, [(i, (i + by) % peers) for i in range(peers)])


def extended(cells, sides, width):
    for axis, dim in sides:
        count = lax.axis_size(axis)
        ends = count - 1
        head = lax.slice_in_dim(cells, 0, width, axis=dim)
        tail = lax.slice_in_dim(cells, cells.shape[dim] - width, cells.shape[dim], axis=dim)
        cells = jnp.concatenate(
            [
                lax.ppermute(tail, axis, [(i, (i + 1) % count) for i in range(ends)]),
                cells,
                lax.ppermute(head, axis, [((i + 1) % count, i) for i in range(ends)]),
            ],
            axis=dim,
        )
    return cells


def to_heads(tensor, head_count):
    return tensor.reshape(
        tensor.shape[0], tensor.shape[1], head_count, tensor.shape[2] // head_count
    )


def from_heads(tensor):
    return tensor.reshape(tensor.shape[0], tensor.shape[1], tensor.shape[2] * tensor.shape[3])


def layer_norm(rows, gain):
    centre = jnp.mean(rows, axis=-1, keepdims=True)
    centred = rows - centre
    inv_scale = lax.rsqrt(jnp.mean(centred * centred, axis=-1, keepdims=True) + EPSILON)
    normed = centred * inv_scale
    return (normed * gain, normed, inv_scale)


def layer_norm_back(grad_scaled, normed, inv_scale, gain):
    grad_normed = grad_scaled * gain
    first_mean = jnp.mean(grad_normed, axis=-1, keepdims=True)
    second_mean = jnp.mean(grad_normed * normed, axis=-1, keepdims=True)
    grad_rows = inv_scale * (grad_normed - first_mean - normed * second_mean)
    grad_gain = jnp.sum((grad_scaled * normed).reshape(-1, normed.shape[-1]), axis=0)
    return (grad_rows, grad_gain)


def depthwise(padded, taps, count):
    total = jnp.zeros((padded.shape[0], count, padded.shape[2]), jnp.float32)
    for offset in range(taps.shape[0]):
        total = total + padded[:, offset : offset + count, :].astype(jnp.float32) * taps[offset]
    return total


def kernel_grad(padded, grad_conv, count, tap_count):
    rows_list = []
    for offset in range(tap_count):
        product = padded[:, offset : offset + count, :].astype(jnp.float32) * grad_conv
        rows_list.append(jnp.sum(product.reshape(-1, grad_conv.shape[2]), axis=0))
    return jnp.stack(rows_list)


def key_mask(lengths, anchor, frames):
    positions = anchor * frames + jnp.arange(frames, dtype=jnp.int32)
    return positions[None, :] < lengths[:, None]


def block_scores(query_heads, key_block, valid_keys, score_scale):
    key_heads = to_heads(key_block, query_heads.shape[2])
    scores = (
        jnp.einsum("uqhd,ukhd->uhqk", query_heads, key_heads, preferred_element_type=jnp.float32)
        * score_scale
    )
    return jnp.where(valid_keys[:, None, None, :], scores, NEG_FILL)


def absorb(soft_state, query_heads, pair_block, valid_keys, score_scale):
    running_max, running_total, running_sum = soft_state
    scores = block_scores(query_heads, pair_block[0], valid_keys, score_scale)
    new_max = jnp.maximum(running_max, jnp.max(scores, axis=-1))
    weights = jnp.exp(scores - new_max[..., None]) * valid_keys[:, None, None, :].astype(
        jnp.float32
    )
    rescale = jnp.exp(running_max - new_max)
    value_heads = to_heads(pair_block[1], query_heads.shape[2])
    product = jnp.einsum(
        "uhqk,ukhd->uhqd",
        weights.astype(jnp.bfloat16),
        value_heads,
        preferred_element_type=jnp.float32,
    )
    return (
        new_max,
        running_total * rescale + jnp.sum(weights, axis=-1),
        running_sum * rescale[..., None] + product,
    )


def block_grads(query_heads, grad_heads, log_total, delta, pair_block, valid_keys, score_scale):
    head_count = query_heads.shape[2]
    scores = block_scores(query_heads, pair_block[0], valid_keys, score_scale)
    probs = jnp.where(valid_keys[:, None, None, :], jnp.exp(scores - log_total[..., None]), 0.0)
    key_heads = to_heads(pair_block[0], head_count)
    value_heads = to_heads(pair_block[1], head_count)
    value_grad = jnp.einsum(
        "uhqk,uqhd->ukhd",
        probs.astype(jnp.bfloat16),
        grad_heads,
        preferred_element_type=jnp.float32,
    )
    prob_grad = jnp.einsum(
        "uqhd,ukhd->uhqk", grad_heads, value_heads, preferred_element_type=jnp.float32
    )
    score_grad = (probs * (prob_grad - delta[..., None]) * score_scale).astype(jnp.bfloat16)
    query_grad = jnp.einsum(
        "uhqk,ukhd->uqhd", score_grad, key_heads, preferred_element_type=jnp.float32
    )
    key_grad = jnp.einsum(
        "uhqk,uqhd->ukhd", score_grad, query_heads, preferred_element_type=jnp.float32
    )
    return (query_grad, jnp.stack([from_heads(key_grad), from_heads(value_grad)]))


def fresh_state(utterances, head_count, count):
    return (
        jnp.full((utterances, head_count, count), NEG_FILL, jnp.float32),
        jnp.zeros((utterances, head_count, count), jnp.float32),
        jnp.zeros((utterances, head_count, count, HEAD_DIM), jnp.float32),
    )


def local(
    residual_in,
    query_rows,
    key_rows,
    value_rows,
    lengths,
    out_weight,
    norm_gain,
    conv_kernel,
    conv_bias,
    conv_gain,
    point_weight,
    grad_out,
):
    loop_size = lax.axis_size("ctx")
    own_index = lax.axis_index("ctx")
    utterances, frames, model_width = residual_in.shape
    score_scale = HEAD_DIM ** (-0.5)
    rim_width = (conv_kernel.shape[0] - 1) // 2
    frame_valid = key_mask(lengths, own_index, frames)
    valid_rows = frame_valid[..., None].astype(jnp.float32)
    query_heads = to_heads(query_rows, HEADS)
    local_pair = jnp.stack([key_rows, value_rows])
    kept_pairs = jnp.zeros((loop_size,) + local_pair.shape, jnp.bfloat16)

    def forward_turn(turn_index, loop_state):
        soft_state, pair_block, kept_blocks = loop_state
        anchor = (own_index - turn_index) % loop_size
        soft_state = absorb(
            soft_state, query_heads, pair_block, key_mask(lengths, anchor, frames), score_scale
        )
        kept_blocks = lax.dynamic_update_index_in_dim(kept_blocks, pair_block, anchor, 0)
        pair_block = passed_along(pair_block, "ctx", 1)
        return (soft_state, pair_block, kept_blocks)

    soft_state, pair_block, kept_pairs = lax.fori_loop(
        0,
        loop_size - 1,
        forward_turn,
        (fresh_state(utterances, HEADS, frames), local_pair, kept_pairs),
    )
    last_anchor = (own_index + 1) % loop_size
    running_max, running_total, running_sum = absorb(
        soft_state, query_heads, pair_block, key_mask(lengths, last_anchor, frames), score_scale
    )
    kept_pairs = lax.dynamic_update_index_in_dim(kept_pairs, pair_block, last_anchor, 0)
    attended = from_heads(
        jnp.transpose(running_sum / running_total[..., None], (0, 2, 1, 3))
    ).astype(jnp.bfloat16)
    log_total = running_max + jnp.log(running_total)
    mixed = residual_in.astype(jnp.float32) + jnp.einsum(
        "ufa,ad->ufd", attended, out_weight, preferred_element_type=jnp.float32
    )
    scaled_one, normed_one, inv_one = layer_norm(mixed, norm_gain)
    conv_in = (scaled_one * valid_rows).astype(jnp.bfloat16)
    conv_padded = extended(conv_in, (("ctx", 1),), rim_width)
    conv_sum = depthwise(conv_padded, conv_kernel, frames) + conv_bias
    scaled_two, normed_two, inv_two = layer_norm(conv_sum, conv_gain)
    gate_value = jax.nn.sigmoid(scaled_two)
    conv_act = (scaled_two * gate_value).astype(jnp.bfloat16)
    block_out = (
        mixed
        + jnp.einsum("ufd,de->ufe", conv_act, point_weight, preferred_element_type=jnp.float32)
    ).astype(jnp.bfloat16)
    grad_masked = jnp.where(frame_valid[..., None], grad_out, jnp.zeros_like(grad_out))
    grad_act = jnp.einsum(
        "ufe,de->ufd", grad_masked, point_weight, preferred_element_type=jnp.float32
    )
    point_term = jnp.einsum(
        "ufd,ufe->de", conv_act, grad_masked, preferred_element_type=jnp.float32
    )
    grad_scaled_two = grad_act * gate_value * (1.0 + scaled_two * (1.0 - gate_value))
    grad_conv, conv_gain_term = layer_norm_back(grad_scaled_two, normed_two, inv_two, conv_gain)
    bias_term = jnp.sum(grad_conv.reshape(-1, model_width), axis=0)
    kernel_term = kernel_grad(conv_padded, grad_conv, frames, conv_kernel.shape[0])
    grad_conv_low = grad_conv.astype(jnp.bfloat16)
    grad_padded = extended(grad_conv_low, (("ctx", 1),), rim_width)
    grad_conv_in = depthwise(grad_padded, conv_kernel[::-1], frames) * valid_rows
    grad_mixed, norm_gain_term = layer_norm_back(grad_conv_in, normed_one, inv_one, norm_gain)
    vector_term = jnp.stack([bias_term, norm_gain_term, conv_gain_term])
    grad_residual = (grad_masked.astype(jnp.float32) + grad_mixed).astype(jnp.bfloat16)
    out_term = jnp.einsum(
        "ufa,ufd->ad", attended, grad_residual, preferred_element_type=jnp.float32
    )
    grad_attended = jnp.einsum(
        "ufd,ad->ufa", grad_residual, out_weight, preferred_element_type=jnp.float32
    ).astype(jnp.bfloat16)
    grad_heads = to_heads(grad_attended, HEADS)
    attended_heads = to_heads(attended, HEADS)
    delta = jnp.einsum(
        "uqhd,uqhd->uhq", grad_heads, attended_heads, preferred_element_type=jnp.float32
    )
    query_total = jnp.zeros((utterances, frames, HEADS, HEAD_DIM), jnp.float32)
    empty_totals = jnp.zeros((2,) + key_rows.shape, jnp.float32)

    def keep_turn(turn_index, loop_state):
        query_sum, key_totals = loop_state
        anchor = (own_index - turn_index) % loop_size
        stored_pair = lax.dynamic_index_in_dim(kept_pairs, anchor, 0, keepdims=False)
        query_grad, key_pair = block_grads(
            query_heads,
            grad_heads,
            log_total,
            delta,
            stored_pair,
            key_mask(lengths, anchor, frames),
            score_scale,
        )
        key_totals = passed_along((key_totals + key_pair).astype(jnp.bfloat16), "ctx", 1).astype(
            jnp.float32
        )
        return (query_sum + query_grad, key_totals)

    query_total, key_totals = lax.fori_loop(0, loop_size, keep_turn, (query_total, empty_totals))
    grad_query = from_heads(query_total).astype(jnp.bfloat16)
    grad_key = key_totals[0].astype(jnp.bfloat16)
    grad_value = key_totals[1].astype(jnp.bfloat16)
    summed = (
        lax.psum_scatter(out_term, ("dp", "ctx"), scatter_dimension=1, tiled=True),
        lax.psum_scatter(point_term, ("dp", "ctx"), scatter_dimension=1, tiled=True),
        lax.psum_scatter(kernel_term, ("dp", "ctx"), scatter_dimension=1, tiled=True),
        lax.psum_scatter(vector_term, ("dp", "ctx"), scatter_dimension=1, tiled=True),
    )
    return (
        block_out,
        grad_residual,
        grad_query,
        grad_key,
        grad_value,
        summed[0],
        summed[1],
        summed[2],
        summed[3],
    )


def solution(mesh):
    in_specs = (
        P("dp", "ctx", None),
        P("dp", "ctx", None),
        P("dp", "ctx", None),
        P("dp", "ctx", None),
        P("dp"),
        P(),
        P(),
        P(),
        P(),
        P(),
        P(),
        P("dp", "ctx", None),
    )
    out_specs = (
        P("dp", "ctx", None),
        P("dp", "ctx", None),
        P("dp", "ctx", None),
        P("dp", "ctx", None),
        P("dp", "ctx", None),
        P(None, ("dp", "ctx")),
        P(None, ("dp", "ctx")),
        P(None, ("dp", "ctx")),
        P(None, ("dp", "ctx")),
    )
    return jax.shard_map(local, mesh=mesh, in_specs=in_specs, out_specs=out_specs, check_vma=False)
```

profile of v0, /device:TPU:0, one launch (start us, length us, event | category | flops | bytes accessed | tf_op | source)
XLA Modules:
  0.0 1212.0 jit_solution(15232652534209796397)
XLA Ops:
  14.5 132.4 %while.42 = (s32[]{:T(128)}, f32[1,24,128]{2,1,0:T(8,128)}, f32[1,24,128]{2,1,0:T(8,128)}, f32[1,24,128,64]{2,3,1,0:T(8,128)}, bf16[2,1,128,1536]{2,3,1,0:T(8,12...) while((s32[]{:T(128)}, f32[1,24,128]{2,1,0:T(8,128)}, ...), condition=%wide.region_3.4_spmd.clone, body=%wide.region_0.3_spmd.clone.sunk | while | flops 104810896 | bytes 15681728 | solution.py:182
  24.8 11.2 collective-permute-done
  45.7 11.0 collective-permute-done
  66.4 10.1 collective-permute-done
  86.1 9.1 collective-permute-done
  104.9 8.2 collective-permute-done
  122.8 8.0 collective-permute-done
  140.5 6.4 collective-permute-done
  162.7 6.8 fusion.166
  186.7 5.2 fusion.156
  192.4 6.2 multiply_reduce_fusion.1
  200.7 5.1 fusion.153
  205.8 401.9 %fusion.164 = (f32[1536,16]{0,1:T(8,128)}, f32[1536,16]{0,1:T(8,128)S(1)}) fusion(f32[1536,1536]{0,1:T(8,128)} %fusion.153, f32[1536,1536]{0,1:T(8,128)} %fusion.156), kind=kCustom, calls=%all-reduce-scatter.2 | all-reduce-scatter fusion | flops 6291457 | bytes 19070976
  614.2 6.6 collective-permute-start.69
  624.0 201.1 %while.43 = (s32[]{:T(128)}, f32[1,128,24,64]{1,3,2,0:T(8,128)}, f32[2,1,128,1536]{2,3,1,0:T(8,128)S(1)}, s32[]{:T(128)}, bf16[8,2,1,128,1536]{3,4,2,1,0:T(8,128...) while((s32[]{:T(128)}, f32[1,128,24,64]{1,3,2,0:T(8,128)}, ...), condition=%wide.region_15.16_spmd.clone, body=%wide.region_14.15_spmd.clone.sunk | while | flops 257556752 | bytes 24060592 | solution.py:260
  632.0 19.0 %collective-permute-done.1 = bf16[2,1,128,1536]{2,3,1,0:T(8,128)(2,1)} collective-permute-done((bf16[2,1,128,1536]{2,3,1,0:T(8,128)(2,1)}, bf16[2,1,128,1536]{2,3,1,0:T(8,128)(2,1)}, u32[]{:S(2)}, u32[]{:S(2)}) %collective-permute-start.1) | collective-permute-done | bytes 786464 | tf_op jit(solution)/shard_map/while/body/eval_jaxpr/ppermute | solution.py:16
  659.9 18.5 %collective-permute-done.1 = bf16[2,1,128,1536]{2,3,1,0:T(8,128)(2,1)} collective-permute-done((bf16[2,1,128,1536]{2,3,1,0:T(8,128)(2,1)}, bf16[2,1,128,1536]{2,3,1,0:T(8,128)(2,1)}, u32[]{:S(2)}, u32[]{:S(2)}) %collective-permute-start.1) | collective-permute-done | bytes 786464 | tf_op jit(solution)/shard_map/while/body/eval_jaxpr/ppermute | solution.py:16
  687.4 17.6 %collective-permute-done.1 = bf16[2,1,128,1536]{2,3,1,0:T(8,128)(2,1)} collective-permute-done((bf16[2,1,128,1536]{2,3,1,0:T(8,128)(2,1)}, bf16[2,1,128,1536]{2,3,1,0:T(8,128)(2,1)}, u32[]{:S(2)}, u32[]{:S(2)}) %collective-permute-start.1) | collective-permute-done | bytes 786464 | tf_op jit(solution)/shard_map/while/body/eval_jaxpr/ppermute | solution.py:16
  713.9 16.7 %collective-permute-done.1 = bf16[2,1,128,1536]{2,3,1,0:T(8,128)(2,1)} collective-permute-done((bf16[2,1,128,1536]{2,3,1,0:T(8,128)(2,1)}, bf16[2,1,128,1536]{2,3,1,0:T(8,128)(2,1)}, u32[]{:S(2)}, u32[]{:S(2)}) %collective-permute-start.1) | collective-permute-done | bytes 786464 | tf_op jit(solution)/shard_map/while/body/eval_jaxpr/ppermute | solution.py:16
  739.5 15.8 %collective-permute-done.1 = bf16[2,1,128,1536]{2,3,1,0:T(8,128)(2,1)} collective-permute-done((bf16[2,1,128,1536]{2,3,1,0:T(8,128)(2,1)}, bf16[2,1,128,1536]{2,3,1,0:T(8,128)(2,1)}, u32[]{:S(2)}, u32[]{:S(2)}) %collective-permute-start.1) | collective-permute-done | bytes 786464 | tf_op jit(solution)/shard_map/while/body/eval_jaxpr/ppermute | solution.py:16
  764.2 14.8 %collective-permute-done.1 = bf16[2,1,128,1536]{2,3,1,0:T(8,128)(2,1)} collective-permute-done((bf16[2,1,128,1536]{2,3,1,0:T(8,128)(2,1)}, bf16[2,1,128,1536]{2,3,1,0:T(8,128)(2,1)}, u32[]{:S(2)}, u32[]{:S(2)}) %collective-permute-start.1) | collective-permute-done | bytes 786464 | tf_op jit(solution)/shard_map/while/body/eval_jaxpr/ppermute | solution.py:16
  788.0 13.9 %collective-permute-done.1 = bf16[2,1,128,1536]{2,3,1,0:T(8,128)(2,1)} collective-permute-done((bf16[2,1,128,1536]{2,3,1,0:T(8,128)(2,1)}, bf16[2,1,128,1536]{2,3,1,0:T(8,128)(2,1)}, u32[]{:S(2)}, u32[]{:S(2)}) %collective-permute-start.1) | collective-permute-done | bytes 786464 | tf_op jit(solution)/shard_map/while/body/eval_jaxpr/ppermute | solution.py:16
  810.8 13.0 %collective-permute-done.1 = bf16[2,1,128,1536]{2,3,1,0:T(8,128)(2,1)} collective-permute-done((bf16[2,1,128,1536]{2,3,1,0:T(8,128)(2,1)}, bf16[2,1,128,1536]{2,3,1,0:T(8,128)(2,1)}, u32[]{:S(2)}, u32[]{:S(2)}) %collective-permute-start.1) | collective-permute-done | bytes 786464 | tf_op jit(solution)/shard_map/while/body/eval_jaxpr/ppermute | solution.py:16
  827.7 10.5 collective-permute-start.32
  876.5 5.6 collective-permute-start.16
  961.4 66.0 %all-reduce.3 = f32[3,1536]{1,0:T(4,128)S(1)} all-reduce(f32[3,1536]{1,0:T(4,128)S(1)} %pad_maximum_fusion.5), channel_id=5, replica_groups=mesh['dp'=16,'ctx'=8] {'dp','ctx'}, use_global_device_ids=true, to_apply=%region_53.54.clone | all-reduce | flops 4608 | bytes 36864
  1040.3 8.9 collective-permute-start.48
  1052.0 5.4 collective-permute-start.46
  1063.3 5.1 collective-permute-start.43
  1068.4 11.8 all-reduce.9.cloned.1.call-done
  1081.9 52.1 %concatenate.74 = f32[1536,524]{0,1:T(8,128)} concatenate(f32[1536,12]{0,1:T(8,128)} %collective-permute-done.37, f32[1536,16]{0,1:T(8,128)} %collective-permute-done.36, f32[1536,16]{0,1:T(8,128)} %collective-permute-done.35, f32[1536,16]{0,1:T(8,128)S(1)} %collective-permute-done.34, f32[1536,16]{0,1:T(8,128)S(1)} %collective-permute-done.33, ...), dimensions={1} | concatenate | bytes 6438912
  1151.9 51.4 %concatenate.75 = f32[1536,524]{0,1:T(8,128)} concatenate(f32[1536,12]{0,1:T(8,128)} %collective-permute-done.69, f32[1536,16]{0,1:T(8,128)S(1)} %copy-done.33, f32[1536,16]{0,1:T(8,128)} %collective-permute-done.67, f32[1536,16]{0,1:T(8,128)} %collective-permute-done.66, f32[1536,16]{0,1:T(8,128)} %collective-permute-done.65, f32[1536,16]{0,1:T(8,128)} %collective-permute-done.64, ...), dimensions={1} | concatenate | bytes 6438912
  (691 shorter events, 350.8 us)
Async XLA Ops:
  7.2 1073.0 %all-reduce.9.cloned.1.call-start = ((), (), s32[]{:S(2)}) async-start(), calls=%async_computation | async-start | bytes 393216
  14.6 21.5 %collective-permute-start = (bf16[2,1,128,1536]{2,3,1,0:T(8,128)(2,1)S(1)}, bf16[2,1,128,1536]{2,3,1,0:T(8,128)(2,1)S(1)}, u32[]{:S(2)}, u32[]{:S(2)}) collective-permute-start(bf16[2,1,128,1536]{2,3,1,0:T(8,128)(2,1)S(1)} %copy.81), channel_id=1, source_target_pairs={{0,1},{1,2},{2,3},{3,4},{4,5},{5,6},{6,7},{7,0},{8,9},{9,10},{10,1... | collective-permute-start | bytes 2359304 | tf_op jit(solution)/shard_map/while/body/eval_jaxpr/ppermute | solution.py:16
  36.1 20.6 %collective-permute-start = (bf16[2,1,128,1536]{2,3,1,0:T(8,128)(2,1)S(1)}, bf16[2,1,128,1536]{2,3,1,0:T(8,128)(2,1)S(1)}, u32[]{:S(2)}, u32[]{:S(2)}) collective-permute-start(bf16[2,1,128,1536]{2,3,1,0:T(8,128)(2,1)S(1)} %copy.81), channel_id=1, source_target_pairs={{0,1},{1,2},{2,3},{3,4},{4,5},{5,6},{6,7},{7,0},{8,9},{9,10},{10,1... | collective-permute-start | bytes 2359304 | tf_op jit(solution)/shard_map/while/body/eval_jaxpr/ppermute | solution.py:16
  56.8 19.7 %collective-permute-start = (bf16[2,1,128,1536]{2,3,1,0:T(8,128)(2,1)S(1)}, bf16[2,1,128,1536]{2,3,1,0:T(8,128)(2,1)S(1)}, u32[]{:S(2)}, u32[]{:S(2)}) collective-permute-start(bf16[2,1,128,1536]{2,3,1,0:T(8,128)(2,1)S(1)} %copy.81), channel_id=1, source_target_pairs={{0,1},{1,2},{2,3},{3,4},{4,5},{5,6},{6,7},{7,0},{8,9},{9,10},{10,1... | collective-permute-start | bytes 2359304 | tf_op jit(solution)/shard_map/while/body/eval_jaxpr/ppermute | solution.py:16
  609.3 229.0 %collective-permute-start.36 = (f32[1536,16]{0,1:T(8,128)}, f32[1536,16]{0,1:T(8,128)}, u32[]{:S(2)}, u32[]{:S(2)}) collective-permute-start(f32[1536,16]{0,1:T(8,128)} %get-tuple-element.685), channel_id=1, source_target_pairs={{0,31},{1,32},{2,33},{3,34},{4,35},{5,36},{6,37},{7,38},{8,39},{9,... | collective-permute-start | bytes 294920
  611.2 229.0 %collective-permute-start.35 = (f32[1536,16]{0,1:T(8,128)}, f32[1536,16]{0,1:T(8,128)}, u32[]{:S(2)}, u32[]{:S(2)}) collective-permute-start(f32[1536,16]{0,1:T(8,128)} %get-tuple-element.685), channel_id=1, source_target_pairs={{0,30},{1,31},{2,32},{3,33},{4,34},{5,35},{6,36},{7,37},{8,38},{9,... | collective-permute-start | bytes 294920
  614.2 212.2 %collective-permute-start.69 = (f32[1536,12]{0,1:T(8,128)}, f32[1536,12]{0,1:T(8,128)}, u32[]{:S(2)}, u32[]{:S(2)}) collective-permute-start(f32[1536,12]{0,1:T(8,128)} %slice.716), channel_id=1, source_target_pairs={{0,32},{1,33},{2,34},{3,35},{4,36},{5,37},{6,38},{7,39},{8,40},{9,... | collective-permute-start | bytes 221192
  620.8 206.9 %collective-permute-start.37 = (f32[1536,12]{0,1:T(8,128)}, f32[1536,12]{0,1:T(8,128)}, u32[]{:S(2)}, u32[]{:S(2)}) collective-permute-start(f32[1536,12]{0,1:T(8,128)} %slice.715), channel_id=1, source_target_pairs={{0,32},{1,33},{2,34},{3,35},{4,36},{5,37},{6,38},{7,39},{8,40},{9,... | collective-permute-start | bytes 221192
  629.2 21.7 %collective-permute-start.1 = (bf16[2,1,128,1536]{2,3,1,0:T(8,128)(2,1)}, bf16[2,1,128,1536]{2,3,1,0:T(8,128)(2,1)}, u32[]{:S(2)}, u32[]{:S(2)}) collective-permute-start(bf16[2,1,128,1536]{2,3,1,0:T(8,128)(2,1)} %fusion.237), channel_id=1, source_target_pairs={{0,1},{1,2},{2,3},{3,4},{4,5},{5,6},{6,7},{7,0},{8,9},{9,10},{10,1... | collective-permute-start | bytes 2359304 | tf_op jit(solution)/shard_map/while/body/eval_jaxpr/ppermute | solution.py:16
  657.5 20.9 %collective-permute-start.1 = (bf16[2,1,128,1536]{2,3,1,0:T(8,128)(2,1)}, bf16[2,1,128,1536]{2,3,1,0:T(8,128)(2,1)}, u32[]{:S(2)}, u32[]{:S(2)}) collective-permute-start(bf16[2,1,128,1536]{2,3,1,0:T(8,128)(2,1)} %fusion.237), channel_id=1, source_target_pairs={{0,1},{1,2},{2,3},{3,4},{4,5},{5,6},{6,7},{7,0},{8,9},{9,10},{10,1... | collective-permute-start | bytes 2359304 | tf_op jit(solution)/shard_map/while/body/eval_jaxpr/ppermute | solution.py:16
  685.0 20.0 %collective-permute-start.1 = (bf16[2,1,128,1536]{2,3,1,0:T(8,128)(2,1)}, bf16[2,1,128,1536]{2,3,1,0:T(8,128)(2,1)}, u32[]{:S(2)}, u32[]{:S(2)}) collective-permute-start(bf16[2,1,128,1536]{2,3,1,0:T(8,128)(2,1)} %fusion.237), channel_id=1, source_target_pairs={{0,1},{1,2},{2,3},{3,4},{4,5},{5,6},{6,7},{7,0},{8,9},{9,10},{10,1... | collective-permute-start | bytes 2359304 | tf_op jit(solution)/shard_map/while/body/eval_jaxpr/ppermute | solution.py:16
  827.7 21.7 %collective-permute-start.32 = (f32[1536,16]{0,1:T(8,128)}, f32[1536,16]{0,1:T(8,128)S(1)}, u32[]{:S(2)}, u32[]{:S(2)}) collective-permute-start(f32[1536,16]{0,1:T(8,128)} %get-tuple-element.685), channel_id=1, source_target_pairs={{0,27},{1,28},{2,29},{3,30},{4,31},{5,32},{6,33},{7,34},{8,35},{9,... | collective-permute-start | bytes 294920
  884.5 19.9 %collective-permute-start.14 = (f32[1536,16]{0,1:T(8,128)}, f32[1536,16]{0,1:T(8,128)S(1)}, u32[]{:S(2)}, u32[]{:S(2)}) collective-permute-start(f32[1536,16]{0,1:T(8,128)} %get-tuple-element.685), channel_id=1, source_target_pairs={{0,9},{1,10},{2,11},{3,12},{4,13},{5,14},{6,15},{7,16},{8,17},{9,1... | collective-permute-start | bytes 294920
  887.1 21.2 %collective-permute-start.13 = (f32[1536,16]{0,1:T(8,128)}, f32[1536,16]{0,1:T(8,128)S(1)}, u32[]{:S(2)}, u32[]{:S(2)}) collective-permute-start(f32[1536,16]{0,1:T(8,128)} %get-tuple-element.685), channel_id=1, source_target_pairs={{0,8},{1,9},{2,10},{3,11},{4,12},{5,13},{6,14},{7,15},{8,16},{9,17... | collective-permute-start | bytes 294920
  888.4 23.8 %collective-permute-start.12 = (f32[1536,16]{0,1:T(8,128)}, f32[1536,16]{0,1:T(8,128)S(1)}, u32[]{:S(2)}, u32[]{:S(2)}) collective-permute-start(f32[1536,16]{0,1:T(8,128)} %get-tuple-element.685), channel_id=1, source_target_pairs={{0,7},{1,8},{2,9},{3,10},{4,11},{5,12},{6,13},{7,14},{8,15},{9,16}... | collective-permute-start | bytes 294920
  891.8 24.4 %collective-permute-start.11 = (f32[1536,16]{0,1:T(8,128)}, f32[1536,16]{0,1:T(8,128)S(1)}, u32[]{:S(2)}, u32[]{:S(2)}) collective-permute-start(f32[1536,16]{0,1:T(8,128)} %get-tuple-element.685), channel_id=1, source_target_pairs={{0,6},{1,7},{2,8},{3,9},{4,10},{5,11},{6,12},{7,13},{8,14},{9,15},... | collective-permute-start | bytes 294920
  896.1 21.6 %collective-permute-start.10 = (f32[1536,16]{0,1:T(8,128)}, f32[1536,16]{0,1:T(8,128)S(1)}, u32[]{:S(2)}, u32[]{:S(2)}) collective-permute-start(f32[1536,16]{0,1:T(8,128)} %get-tuple-element.685), channel_id=1, source_target_pairs={{0,5},{1,6},{2,7},{3,8},{4,9},{5,10},{6,11},{7,12},{8,13},{9,14},{... | collective-permute-start | bytes 294920
  948.0 79.4 %collective-permute-start.57 = (f32[1536,16]{0,1:T(8,128)S(1)}, f32[1536,16]{0,1:T(8,128)S(1)}, u32[]{:S(2)}, u32[]{:S(2)}) collective-permute-start(f32[1536,16]{0,1:T(8,128)S(1)} %copy-done.13), channel_id=1, source_target_pairs={{0,20},{1,21},{2,22},{3,23},{4,24},{5,25},{6,26},{7,27},{8,28},{9,... | collective-permute-start | bytes 294920
  950.6 80.0 %collective-permute-start.56 = (f32[1536,16]{0,1:T(8,128)S(1)}, f32[1536,16]{0,1:T(8,128)S(1)}, u32[]{:S(2)}, u32[]{:S(2)}) collective-permute-start(f32[1536,16]{0,1:T(8,128)S(1)} %copy-done.13), channel_id=1, source_target_pairs={{0,19},{1,20},{2,21},{3,22},{4,23},{5,24},{6,25},{7,26},{8,27},{9,... | collective-permute-start | bytes 294920
  954.0 81.4 %collective-permute-start.55 = (f32[1536,16]{0,1:T(8,128)S(1)}, f32[1536,16]{0,1:T(8,128)S(1)}, u32[]{:S(2)}, u32[]{:S(2)}) collective-permute-start(f32[1536,16]{0,1:T(8,128)S(1)} %copy-done.13), channel_id=1, source_target_pairs={{0,18},{1,19},{2,20},{3,21},{4,22},{5,23},{6,24},{7,25},{8,26},{9,... | collective-permute-start | bytes 294920
  955.9 82.2 %collective-permute-start.54 = (f32[1536,16]{0,1:T(8,128)S(1)}, f32[1536,16]{0,1:T(8,128)S(1)}, u32[]{:S(2)}, u32[]{:S(2)}) collective-permute-start(f32[1536,16]{0,1:T(8,128)S(1)} %copy-done.13), channel_id=1, source_target_pairs={{0,17},{1,18},{2,19},{3,20},{4,21},{5,22},{6,23},{7,24},{8,25},{9,... | collective-permute-start | bytes 294920
  958.6 81.7 %collective-permute-start.53 = (f32[1536,16]{0,1:T(8,128)S(1)}, f32[1536,16]{0,1:T(8,128)S(1)}, u32[]{:S(2)}, u32[]{:S(2)}) collective-permute-start(f32[1536,16]{0,1:T(8,128)S(1)} %copy-done.13), channel_id=1, source_target_pairs={{0,16},{1,17},{2,18},{3,19},{4,20},{5,21},{6,22},{7,23},{8,24},{9,... | collective-permute-start | bytes 294920
  1027.4 22.4 %collective-permute-start.52 = (f32[1536,16]{0,1:T(8,128)S(1)}, f32[1536,16]{0,1:T(8,128)S(1)}, u32[]{:S(2)}, u32[]{:S(2)}) collective-permute-start(f32[1536,16]{0,1:T(8,128)S(1)} %copy-done.13), channel_id=1, source_target_pairs={{0,15},{1,16},{2,17},{3,18},{4,19},{5,20},{6,21},{7,22},{8,23},{9,... | collective-permute-start | bytes 294920
  1030.6 21.3 %collective-permute-start.51 = (f32[1536,16]{0,1:T(8,128)S(1)}, f32[1536,16]{0,1:T(8,128)S(1)}, u32[]{:S(2)}, u32[]{:S(2)}) collective-permute-start(f32[1536,16]{0,1:T(8,128)S(1)} %copy-done.13), channel_id=1, source_target_pairs={{0,14},{1,15},{2,16},{3,17},{4,18},{5,19},{6,20},{7,21},{8,22},{9,... | collective-permute-start | bytes 294920
  1035.4 22.0 %collective-permute-start.50 = (f32[1536,16]{0,1:T(8,128)S(1)}, f32[1536,16]{0,1:T(8,128)S(1)}, u32[]{:S(2)}, u32[]{:S(2)}) collective-permute-start(f32[1536,16]{0,1:T(8,128)S(1)} %copy-done.13), channel_id=1, source_target_pairs={{0,13},{1,14},{2,15},{3,16},{4,17},{5,18},{6,19},{7,20},{8,21},{9,... | collective-permute-start | bytes 294920
  1038.1 21.2 %collective-permute-start.49 = (f32[1536,16]{0,1:T(8,128)S(1)}, f32[1536,16]{0,1:T(8,128)S(1)}, u32[]{:S(2)}, u32[]{:S(2)}) collective-permute-start(f32[1536,16]{0,1:T(8,128)S(1)} %copy-done.13), channel_id=1, source_target_pairs={{0,12},{1,13},{2,14},{3,15},{4,16},{5,17},{6,18},{7,19},{8,20},{9,... | collective-permute-start | bytes 294920
  1040.3 23.0 %collective-permute-start.48 = (f32[1536,16]{0,1:T(8,128)S(1)}, f32[1536,16]{0,1:T(8,128)S(1)}, u32[]{:S(2)}, u32[]{:S(2)}) collective-permute-start(f32[1536,16]{0,1:T(8,128)S(1)} %copy-done.13), channel_id=1, source_target_pairs={{0,11},{1,12},{2,13},{3,14},{4,15},{5,16},{6,17},{7,18},{8,19},{9,... | collective-permute-start | bytes 294920
  1049.9 84.2 %collective-permute-start.47 = (f32[1536,16]{0,1:T(8,128)S(1)}, f32[1536,16]{0,1:T(8,128)S(1)}, u32[]{:S(2)}, u32[]{:S(2)}) collective-permute-start(f32[1536,16]{0,1:T(8,128)S(1)} %copy-done.13), channel_id=1, source_target_pairs={{0,10},{1,11},{2,12},{3,13},{4,14},{5,15},{6,16},{7,17},{8,18},{9,... | collective-permute-start | bytes 294920
  1052.0 84.9 %collective-permute-start.46 = (f32[1536,16]{0,1:T(8,128)S(1)}, f32[1536,16]{0,1:T(8,128)}, u32[]{:S(2)}, u32[]{:S(2)}) collective-permute-start(f32[1536,16]{0,1:T(8,128)S(1)} %copy-done.13), channel_id=1, source_target_pairs={{0,9},{1,10},{2,11},{3,12},{4,13},{5,14},{6,15},{7,16},{8,17},{9,1... | collective-permute-start | bytes 294920
  1057.4 81.5 %collective-permute-start.45 = (f32[1536,16]{0,1:T(8,128)S(1)}, f32[1536,16]{0,1:T(8,128)}, u32[]{:S(2)}, u32[]{:S(2)}) collective-permute-start(f32[1536,16]{0,1:T(8,128)S(1)} %copy-done.13), channel_id=1, source_target_pairs={{0,8},{1,9},{2,10},{3,11},{4,12},{5,13},{6,14},{7,15},{8,16},{9,17... | collective-permute-start | bytes 294920
  1059.3 83.4 %collective-permute-start.44 = (f32[1536,16]{0,1:T(8,128)S(1)}, f32[1536,16]{0,1:T(8,128)}, u32[]{:S(2)}, u32[]{:S(2)}) collective-permute-start(f32[1536,16]{0,1:T(8,128)S(1)} %copy-done.13), channel_id=1, source_target_pairs={{0,7},{1,8},{2,9},{3,10},{4,11},{5,12},{6,13},{7,14},{8,15},{9,16}... | collective-permute-start | bytes 294920
  1063.3 83.0 %collective-permute-start.43 = (f32[1536,16]{0,1:T(8,128)S(1)}, f32[1536,16]{0,1:T(8,128)}, u32[]{:S(2)}, u32[]{:S(2)}) collective-permute-start(f32[1536,16]{0,1:T(8,128)S(1)} %copy-done.13), channel_id=1, source_target_pairs={{0,6},{1,7},{2,8},{3,9},{4,10},{5,11},{6,12},{7,13},{8,14},{9,15},... | collective-permute-start | bytes 294920
  (207 other events, 5301.3 us)
Sparse Core Ops, SparseCore 0:
  939.1 141.0 all-reduce.8
where the time goes:
time: 1230 us; the launch traced here: 1210 us
  blocking collectives  468 us (38%)
  waiting for transfers between devices  209 us (17%)
  starting transfers between devices  201 us (16%)
  local copies, waits for them, and re-layouts  159 us (13%)
  matrix products  89.9 us (7%)
  other arithmetic  66.5 us (5%)
  between operations  17.8 us (1%)
    unnamed x2, blocking collectives  468 us
    ppermute x15, waiting for transfers between devices, passed_along(): lax.ppermute(shard, axis, [(i, (i + by) % peers) for i in range(peers)])  193 us
    unnamed x65, starting transfers between devices  189 us
    unnamed x265, local copies, waits for them, and re-layouts  116 us
  transfers between devices with their start and end apart: 84, of which 19 were waited for; matrix products, arithmetic and copies ran while one was open for 17% of the time, Pallas kernels for 0%

commit v1 on v0

v1 whole, which is shorter than its diff:
```python
import jax
import jax.numpy as jnp
from jax import lax
from jax.experimental import pallas as pl
from jax.experimental.pallas import tpu as pltpu
from jax.sharding import PartitionSpec as P

N = 8
F = 128
D = 1536
S = 1024
HD = 64
KERN = 31
NB = D // 128
TILE = 256
EPSILON = 1e-05
MASKED = -1e30
MESH = pl.DeviceIdType.MESH
BF = jnp.bfloat16
F32 = jnp.float32


def dot(a, b):
    return jnp.dot(a, b, preferred_element_type=F32)


def dot_nt(a, b):
    return lax.dot_general(a, b, (((1,), (1,)), ((), ())), preferred_element_type=F32)


def iota(shape, dim):
    return lax.broadcasted_iota(jnp.int32, shape, dim)


def kernel(
    len_ref, q_ref, k_ref, v_ref, res_ref, go_ref, wo_hbm, wp_hbm, ng_ref, taps_ref, cb_ref, cg_ref,
    bo_ref, gr_ref, gq_ref, gk_ref, gv_ref, gp_ref, gw_ref, small_ref,
    wo, wp, snd, rcv, kaug, qaug, vta, vaug, pt, inv, obuf, att_t, att, mixed, n1, r1, cin, cp, csum,
    gact, gm, act, gc, gcl, gpad, vacc, lh, rh, dsnd, do, doaug, qz, dz, kt, dst, snd2, rcv2,
    w_sem, s_q, r_q, s_o, r_o, s_d, r_d, s_g, r_g, s_h, r_h,
):
    me = lax.axis_index("ctx")
    dp = lax.axis_index("dp")
    length = len_ref[0]

    def at(offset):
        return lax.rem(me + (offset + N), N)

    wp_copy = pltpu.make_async_copy(wp_hbm, wp, w_sem.at[0])
    wo_copy = pltpu.make_async_copy(wo_hbm, wo, w_sem.at[1])
    wp_copy.start()
    wo_copy.start()

    barrier = pltpu.get_barrier_semaphore()
    for o in range(1, N):
        pl.semaphore_signal(barrier, inc=1, device_id=(dp, at(o)), device_id_type=MESH)

    def exchange(source, target, send_sem, recv_sem, h):
        def copy(o):
            return pltpu.make_async_remote_copy(
                src_ref=source.at[h, at(o)],
                dst_ref=target.at[h, me],
                send_sem=send_sem.at[h, o],
                recv_sem=recv_sem.at[h, o],
                device_id=(dp, at(o)),
                device_id_type=MESH,
            )

        def arrival(o):
            block = target.at[h, at(-o)]
            return pltpu.make_async_remote_copy(
                src_ref=block,
                dst_ref=block,
                send_sem=send_sem.at[h, o],
                recv_sem=recv_sem.at[h, o],
                device_id=(dp, at(-o)),
                device_id_type=MESH,
            )

        def start():
            for o in (4, 3, 5, 2, 6, 1, 7):
                copy(o).start()
            target[h, me] = source[h, me]

        def wait():
            for o in range(1, N):
                arrival(o).wait_recv()

        def drain():
            for o in range(1, N):
                copy(o).wait_send()

        return start, wait, drain

    ex_q = [exchange(snd, rcv, s_q, r_q, h) for h in range(3)]
    ex_o = [exchange(obuf, att_t, s_o, r_o, h) for h in range(3)]
    ex_d = [exchange(dsnd, do, s_d, r_d, h) for h in range(3)]
    ex_g = [exchange(snd2, rcv2, s_g, r_g, h) for h in range(3)]

    for h in range(3):
        for b in range(4):
            cols = slice((4 * h + b) * 128, (4 * h + b + 1) * 128)
            for a, ref in enumerate((q_ref, k_ref, v_ref)):
                block = ref[:, cols]
                if a == 0:
                    block = (block.astype(F32) * 0.125).astype(BF)
                block = block.T
                snd[h, 2 * b, a * HD : (a + 1) * HD, :] = block[:HD]
                snd[h, 2 * b + 1, a * HD : (a + 1) * HD, :] = block[HD:]
        if h == 0:
            pl.semaphore_wait(barrier, N - 1)
        ex_q[h][0]()

    own_valid = me * F + iota((F, 1), 0) < length
    gm[...] = jnp.where(own_valid, go_ref[...], jnp.zeros_like(go_ref))
    wp_copy.wait()

    def act_grad(c, carry):
        cols = pl.ds(pl.multiple_of(c * 256, 256), 256)
        gact[:, cols] = dot_nt(gm[...], wp[cols, :])
        return carry

    lax.fori_loop(0, D // 256, act_grad, 0)

    qaug[HD:, :] = (iota((HD, S), 0) == 0).astype(F32).astype(BF)
    vta[HD:, :] = (iota((16, S), 0) == 0).astype(F32).astype(BF)
    qz[HD:, :] = jnp.zeros((HD, S), BF)
    dz[:HD, :] = jnp.zeros((HD, S), BF)
    doaug[16:HD, :] = jnp.zeros((HD - 16, S), BF)

    for h in range(3):
        ex_q[h][1]()
        lane = iota((F, 128), 1)
        for j in range(N):
            cols = slice(j * F, (j + 1) * F)
            qaug[:HD, cols] = rcv[h, j, :HD, :]
            vta[:HD, cols] = rcv[h, j, 2 * HD :, :]
            both = rcv[h, j, HD:, :].T
            bias = jnp.where(j * F + iota((F, 128), 0) < length, 0.0, MASKED)
            bias = jnp.where(lane == HD, bias, 0.0).astype(BF)
            ones = jnp.where(lane < 2, 1.0, 0.0).astype(BF)
            kaug[cols, :] = jnp.where(lane < HD, both, bias)
            vaug[h, cols, :] = jnp.where(lane < HD, ones, both)

        def attend(i, carry, h=h):
            cols = pl.ds(pl.multiple_of(i * TILE, TILE), TILE)
            scores = dot(kaug[...], qaug[:, cols])
            top = jnp.max(scores, axis=0, keepdims=True)
            weights = jnp.exp(scores - top).astype(BF)
            pt[h, :, cols] = weights
            summed = dot(vta[...], weights)
            scale = 1.0 / summed[HD : HD + 1, :]
            inv[h, :, cols] = scale
            rows = (summed[:HD] * scale).astype(BF)
            for a in range(TILE // F):
                obuf[h, i * (TILE // F) + a] = rows[:, a * F : (a + 1) * F]
            return carry

        lax.fori_loop(0, S // TILE, attend, 0)
        ex_o[h][0]()

    wo_copy.wait()
    for h in range(3):
        ex_o[h][1]()
        for b in range(4):
            pair = jnp.concatenate([att_t[h, 2 * b], att_t[h, 2 * b + 1]], axis=0)
            att[:, (4 * h + b) * 128 : (4 * h + b + 1) * 128] = pair.T

        def project(c, carry, h=h):
            cols = pl.ds(pl.multiple_of(c * 256, 256), 256)
            before = res_ref[:, cols].astype(F32) if h == 0 else mixed[:, cols]
            mixed[:, cols] = before + dot(
                att[:, 512 * h : 512 * (h + 1)], wo[512 * h : 512 * (h + 1), cols]
            )
            return carry

        lax.fori_loop(0, D // 256, project, 0)

    def mean_of(x):
        return jnp.sum(x, axis=1, keepdims=True) * (1.0 / D)

    def first_norm(i, carry):
        rows = pl.ds(pl.multiple_of(i * 16, 16), 16)
        x = mixed[rows, :]
        x = x - mean_of(x)
        r = lax.rsqrt(mean_of(x * x) + EPSILON)
        n = x * r
        n1[rows, :] = n
        r1[rows, :] = r
        valid = me * F + i * 16 + iota((16, 1), 0) < length
        low = jnp.where(valid, n * ng_ref[...], 0.0).astype(BF)
        cin[rows, :] = low
        wide = low.astype(F32)
        for c in range(NB):
            cp[c, pl.ds(pl.multiple_of(16 + i * 16, 16), 16), :] = wide[:, c * 128 : (c + 1) * 128]
        return carry

    lax.fori_loop(0, F // 16, first_norm, 0)

    def edges(buffer, k):
        to_right = pltpu.make_async_remote_copy(
            src_ref=buffer.at[pl.ds(F - 16, 16)],
            dst_ref=lh.at[k],
            send_sem=s_h.at[2 * k],
            recv_sem=r_h.at[2 * k],
            device_id=(dp, at(1)),
            device_id_type=MESH,
        )
        to_left = pltpu.make_async_remote_copy(
            src_ref=buffer.at[pl.ds(0, 16)],
            dst_ref=rh.at[k],
            send_sem=s_h.at[2 * k + 1],
            recv_sem=r_h.at[2 * k + 1],
            device_id=(dp, at(-1)),
            device_id_type=MESH,
        )
        return to_right, to_left

    def place_edges(k, padded):
        left = jnp.where(me > 0, lh[k].astype(F32), 0.0)
        right = jnp.where(me < N - 1, rh[k].astype(F32), 0.0)
        for c in range(NB):
            padded[c, 0:16, :] = left[:, c * 128 : (c + 1) * 128]
            padded[c, F + 16 : F + 32, :] = right[:, c * 128 : (c + 1) * 128]

    halo = edges(cin, 0)
    for copy in halo:
        copy.start()
    for copy in halo:
        copy.wait()
    place_edges(0, cp)

    def convolve(c, carry):
        cols = pl.ds(pl.multiple_of(c * 128, 128), 128)
        total = jnp.broadcast_to(cb_ref[:, cols], (F, 128))
        for t in range(KERN):
            total = total + cp[c, t + 1 : t + 1 + F, :] * taps_ref[t : t + 1, cols]
        csum[:, cols] = total
        return carry

    lax.fori_loop(0, NB, convolve, 0)

    vacc[...] = jnp.zeros_like(vacc)

    def fold(x):
        return x[:8] + x[8:]

    def second_norm(i, carry):
        rows = pl.ds(pl.multiple_of(i * 16, 16), 16)
        x = csum[rows, :]
        x = x - mean_of(x)
        r = lax.rsqrt(mean_of(x * x) + EPSILON)
        n = x * r
        y = n * cg_ref[...]
        g = jax.nn.sigmoid(y)
        act[rows, :] = (y * g).astype(BF)
        back = gact[rows, :] * g * (1.0 + y * (1.0 - g))
        vacc[2] += fold(back * n)
        u = back * cg_ref[...]
        grad = r * (u - mean_of(u) - n * mean_of(u * n))
        vacc[0] += fold(grad)
        low = grad.astype(BF)
        gcl[rows, :] = low
        wide = low.astype(F32)
        for c in range(NB):
            cols = slice(c * 128, (c + 1) * 128)
            gc[c, rows, :] = grad[:, cols]
            gpad[c, pl.ds(pl.multiple_of(16 + i * 16, 16), 16), :] = wide[:, cols]
        return carry

    lax.fori_loop(0, F // 16, second_norm, 0)

    halo2 = edges(gcl, 1)
    for copy in halo2:
        copy.start()

    def block_cols(c, carry):
        cols = pl.ds(pl.multiple_of(c * 256, 256), 256)
        bo_ref[:, cols] = (mixed[:, cols] + dot(act[...], wp[:, cols])).astype(BF)
        return carry

    lax.fori_loop(0, D // 256, block_cols, 0)

    def point_rows(c, carry):
        cols = pl.ds(pl.multiple_of(c * 128, 128), 128)
        gp_ref[cols, :] = dot(gm[:, cols].T, act[...])
        return carry

    lax.fori_loop(0, NB, point_rows, 0)

    for copy in halo2:
        copy.wait()
    place_edges(1, gpad)

    def convolve_back(c, carry):
        cols = pl.ds(pl.multiple_of(c * 128, 128), 128)
        total = jnp.zeros((F, 128), F32)
        for t in range(KERN):
            total = total + gpad[c, KERN - t : KERN - t + F, :] * taps_ref[t : t + 1, cols]
        csum[:, cols] = jnp.where(me * F + iota((F, 1), 0) < length, total, 0.0)
        return carry

    lax.fori_loop(0, NB, convolve_back, 0)

    def first_norm_back(i, carry):
        rows = pl.ds(pl.multiple_of(i * 16, 16), 16)
        x = csum[rows, :]
        n = n1[rows, :]
        vacc[1] += fold(x * n)
        u = x * ng_ref[...]
        grad = r1[rows, :] * (u - mean_of(u) - n * mean_of(u * n))
        gr_ref[rows, :] = (gm[rows, :].astype(F32) + grad).astype(BF)
        return carry

    lax.fori_loop(0, F // 16, first_norm_back, 0)

    for h in range(3):

        def attended_rows(j, carry, h=h):
            for a in range(2):
                rows = pl.ds(pl.multiple_of(512 * h + (2 * j + a) * 128, 128), 128)
                part = dot_nt(wo[rows, :], gr_ref[...]).astype(BF)
                dsnd[h, 4 * j + 2 * a] = part[:HD]
                dsnd[h, 4 * j + 2 * a + 1] = part[HD:]
            return carry

        lax.fori_loop(0, 2, attended_rows, 0)
        ex_d[h][0]()

    def out_rows(c, carry):
        cols = pl.ds(pl.multiple_of(c * 128, 128), 128)
        gw_ref[cols, :] = dot(gr_ref[:, cols].T, att[...])
        return carry

    lax.fori_loop(0, NB, out_rows, 0)

    def tap_rows(c, carry):
        cols = pl.ds(pl.multiple_of(c * 128, 128), 128)
        grad = gc[c]
        for t in range(KERN):
            small_ref[t : t + 1, cols] = jnp.sum(cp[c, t + 1 : t + 1 + F, :] * grad, axis=0, keepdims=True)
        return carry

    lax.fori_loop(0, NB, tap_rows, 0)
    for i in range(3):
        small_ref[KERN + i : KERN + i + 1, :] = jnp.sum(vacc[i], axis=0, keepdims=True)
    small_ref[KERN + 3 :, :] = jnp.zeros((40 - KERN - 3, D), F32)

    for h in range(3):
        ex_d[h][1]()
        row = iota((16, F), 0)
        for j in range(N):
            cols = slice(j * F, (j + 1) * F)
            grad = do[h, j].astype(F32)
            scale = inv[h, :, cols]
            delta = -scale * jnp.sum(grad * obuf[h, j].astype(F32), axis=0, keepdims=True)
            high = delta.astype(BF).astype(F32)
            doaug[:16, cols] = jnp.where(row == 0, high, jnp.where(row == 1, delta - high, 0.0)).astype(BF)
            scaled = (grad * scale).astype(BF)
            doaug[HD:, cols] = scaled
            dz[HD:, cols] = scaled
            qz[:HD, cols] = rcv[h, j, :HD, :]
            kt[:, cols] = rcv[h, j, HD : 2 * HD, :]

        def back_queries(i, carry, h=h):
            cols = pl.ds(pl.multiple_of(i * TILE, TILE), TILE)
            grads = dot(vaug[h], doaug[:, cols])
            grads = (pt[h, :, cols].astype(F32) * grads).astype(BF)
            dst[:, cols] = grads
            rows = (dot(kt[...], grads) * 0.125).astype(BF)
            for a in range(TILE // F):
                snd2[h, i * (TILE // F) + a, :HD] = rows[:, a * F : (a + 1) * F]
            return carry

        lax.fori_loop(0, S // TILE, back_queries, 0)

        def back_keys(j, carry, h=h):
            rows = pl.ds(pl.multiple_of(j * F, F), F)
            both = dot_nt(dst[rows, :], qz[...]) + dot_nt(pt[h, rows, :], dz[...])
            snd2[h, j, HD:] = both.T.astype(BF)
            return carry

        lax.fori_loop(0, N, back_keys, 0)
        ex_g[h][0]()

    for h in range(3):
        ex_g[h][1]()
        for b in range(4):
            cols = slice((4 * h + b) * 128, (4 * h + b + 1) * 128)
            for a, ref in enumerate((gq_ref, gk_ref, gv_ref)):
                part = slice(a * HD, (a + 1) * HD)
                pair = jnp.concatenate([rcv2[h, 2 * b, part], rcv2[h, 2 * b + 1, part]], axis=0)
                ref[:, cols] = pair.T

    for group in (ex_q, ex_o, ex_d, ex_g):
        for h in range(3):
            group[h][2]()


def fused(lengths, q, k, v, res, go, wo, wp, ng, taps, cb, cg):
    vmem = pl.BlockSpec(memory_space=pltpu.VMEM)
    hbm = pl.BlockSpec(memory_space=pl.ANY)
    smem = pl.BlockSpec(memory_space=pltpu.SMEM)
    rows = jax.ShapeDtypeStruct((F, D), BF)
    dma = pltpu.SemaphoreType.DMA
    scratch = [
        pltpu.VMEM((D, D), BF),
        pltpu.VMEM((D, D), BF),
        pltpu.VMEM((3, N, 3 * HD, F), BF),
        pltpu.VMEM((3, N, 3 * HD, F), BF),
        pltpu.VMEM((S, 128), BF),
        pltpu.VMEM((128, S), BF),
        pltpu.VMEM((HD + 16, S), BF),
        pltpu.VMEM((3, S, 128), BF),
        pltpu.VMEM((3, S, S), BF),
        pltpu.VMEM((3, 1, S), F32),
        pltpu.VMEM((3, N, HD, F), BF),
        pltpu.VMEM((3, N, HD, F), BF),
        pltpu.VMEM((F, D), BF),
        pltpu.VMEM((F, D), F32),
        pltpu.VMEM((F, D), F32),
        pltpu.VMEM((F, 1), F32),
        pltpu.VMEM((F, D), BF),
        pltpu.VMEM((NB, F + 32, 128), F32),
        pltpu.VMEM((F, D), F32),
        pltpu.VMEM((F, D), F32),
        pltpu.VMEM((F, D), BF),
        pltpu.VMEM((F, D), BF),
        pltpu.VMEM((NB, F, 128), F32),
        pltpu.VMEM((F, D), BF),
        pltpu.VMEM((NB, F + 32, 128), F32),
        pltpu.VMEM((3, 8, D), F32),
        pltpu.VMEM((2, 16, D), BF),
        pltpu.VMEM((2, 16, D), BF),
        pltpu.VMEM((3, N, HD, F), BF),
        pltpu.VMEM((3, N, HD, F), BF),
        pltpu.VMEM((128, S), BF),
        pltpu.VMEM((128, S), BF),
        pltpu.VMEM((128, S), BF),
        pltpu.VMEM((HD, S), BF),
        pltpu.VMEM((S, S), BF),
        pltpu.VMEM((3, N, 3 * HD, F), BF),
        pltpu.VMEM((3, N, 3 * HD, F), BF),
        dma((2,)),
        dma((3, N)), dma((3, N)),
        dma((3, N)), dma((3, N)),
        dma((3, N)), dma((3, N)),
        dma((3, N)), dma((3, N)),
        dma((4,)), dma((4,)),
    ]
    return pl.pallas_call(
        kernel,
        out_shape=[rows] * 5
        + [
            jax.ShapeDtypeStruct((D, D), F32),
            jax.ShapeDtypeStruct((D, D), F32),
            jax.ShapeDtypeStruct((40, D), F32),
        ],
        in_specs=[smem] + [vmem] * 5 + [hbm] * 2 + [vmem] * 4,
        out_specs=[vmem] * 8,
        scratch_shapes=scratch,
        compiler_params=pltpu.CompilerParams(
            collective_id=0, has_side_effects=True, vmem_limit_bytes=60 * 1024 * 1024
        ),
    )(lengths, q, k, v, res, go, wo, wp, ng, taps, cb, cg)


def local(
    residual_in, query_rows, key_rows, value_rows, lengths, out_weight, norm_gain, conv_kernel,
    conv_bias, conv_gain, point_weight, grad_out,
):
    outs = fused(
        lengths, query_rows[0], key_rows[0], value_rows[0], residual_in[0], grad_out[0],
        out_weight, point_weight, norm_gain[None], conv_kernel, conv_bias[None], conv_gain[None],
    )
    rows = [x[None] for x in outs[:5]]
    point_term, out_term, small = outs[5:]
    axes = ("dp", "ctx")
    out_grad = lax.psum_scatter(out_term, axes, scatter_dimension=0, tiled=True).T
    point_grad = lax.psum_scatter(point_term, axes, scatter_dimension=0, tiled=True).T
    small = lax.psum_scatter(small, axes, scatter_dimension=1, tiled=True)
    return (*rows, out_grad, point_grad, small[:KERN], small[KERN : KERN + 3])


def solution(mesh):
    rows = P("dp", "ctx", None)
    split = P(None, ("dp", "ctx"))
    in_specs = (rows,) * 4 + (P("dp"),) + (P(),) * 6 + (rows,)
    out_specs = (rows,) * 5 + (split,) * 4
    return jax.shard_map(local, mesh=mesh, in_specs=in_specs, out_specs=out_specs, check_vma=False)
```

time: 1230 us -> 820 us (0.67)
  waiting for transfers between devices: 209 us -> 56.3 us
  matrix products: 89.9 us -> 0 us
  Pallas kernels: 0 us -> 88.2 us
  blocking collectives: 468 us -> 385 us
  local copies, waits for them, and re-layouts: 159 us -> 80.2 us
  other arithmetic: 66.5 us -> 0 us
  starting transfers between devices: 201 us -> 187 us
    ppermute x19 -> x0, waiting for transfers between devices: 195 us -> none  [the longest x15 193 us: passed_along(): lax.ppermute(shard, axis, [(i, (i + by) % peers) for i in range(peers)])]
    dot_general x62 -> x0, matrix products: 89.9 us -> none  [the longest x8 18.1 us: absorb(): jnp.einsum('uhqk,ukhd->uhqd', weights.astype(jnp.bfloat16), value_heads,...]
    pallas_call x0 -> x1, Pallas kernels: none -> 88.2 us  [fused(): pl.pallas_call(kernel, out_shape=[rows] * 5 + [jax.ShapeDtypeStruct((D, D...]
    unnamed x2 -> x1, blocking collectives: 468 us -> 385 us
    unnamed x66, waiting for transfers between devices: 13.2 us -> 56.3 us
    unnamed x265 -> x112, local copies, waits for them, and re-layouts: 116 us -> 72.8 us
    reduce_sum x16 -> x0, other arithmetic: 27.3 us -> none  [the longest x4 11.3 us: kernel_grad(): rows_list.append(jnp.sum(product.reshape(-1, grad_conv.shape[2]), axis=0))]
    convert_element_type x27 -> x0, other arithmetic: 24.4 us -> none  [the longest x8 9.89 us: keep_turn(): passed_along((key_totals + key_pair).astype(jnp.bfloat16), 'ctx', 1)]
  transfers between devices with their start and end apart: 84 -> 65, of which waited for: 19 -> 1; matrix products, arithmetic and copies ran while one was open for 17% -> 8% of each run, Pallas kernels for 0% -> 0%
where the time goes in v1:
time: 820 us; the launch traced here: 814 us
  blocking collectives  385 us (47%)
  starting transfers between devices  187 us (23%)
  Pallas kernels  88.2 us (11%)
  local copies, waits for them, and re-layouts  80.2 us (10%)
  waiting for transfers between devices  56.3 us (7%)
  between operations  16.3 us (2%)
    unnamed x1, blocking collectives  385 us
    unnamed x65, starting transfers between devices  187 us
    pallas_call x1, Pallas kernels, fused(): pl.pallas_call(kernel, out_shape=[rows] * 5 + [jax.ShapeDtypeStruct((D, D...  88.2 us
    unnamed x112, local copies, waits for them, and re-layouts  72.8 us
    unnamed x66, waiting for transfers between devices  56.3 us
  transfers between devices with their start and end apart: 65, of which 1 were waited for; matrix products, arithmetic and copies ran while one was open for 8% of the time, Pallas kernels for 0%

profile of v1, /device:TPU:0, one launch (start us, length us, event | category | flops | bytes accessed | tf_op | source)
XLA Modules:
  0.0 813.6 jit_solution(17833685946306089179)
XLA Ops:
  11.8 88.2 %shard_map.187 = (bf16[128,1536]{1,0:T(8,128)(2,1)}, bf16[128,1536]{1,0:T(8,128)(2,1)}, bf16[128,1536]{1,0:T(8,128)(2,1)}, bf16[128,1536]{1,0:T(8,128)(2,1)}, bf...) custom-call(s32[1]{0:T(128)S(6)} %copy.31.len_ref, ...), custom_call_target="tpu_custom_call" | custom-call | tf_op jit(solution)/shard_map/pallas_call | solution.py:451
  100.0 385.2 %fusion.2 = (f32[16,1536]{1,0:T(8,128)S(1)}, f32[16,1536]{1,0:T(8,128)S(1)}) fusion(f32[1536,1536]{1,0:T(8,128)} %get-tuple-element.22, f32[1536,1536]{1,0:T(8,128)} %get-tuple-element.23), kind=kCustom, calls=%all-reduce-scatter.2 | all-reduce-scatter fusion | flops 6291457 | bytes 19070976
  498.9 14.0 %collective-permute-start.40 = (f32[16,1536]{1,0:T(8,128)S(1)}, f32[16,1536]{1,0:T(8,128)S(1)}, u32[]{:S(2)}, u32[]{:S(2)}) collective-permute-start(f32[16,1536]{1,0:T(8,128)S(1)} %get-tuple-element.46), channel_id=1, source_target_pairs={{0,9},{1,10},{2,11},{3,12},{4,13},{5,14},{6,15},{7,16},{8,17},{9,1... | collective-permute-start | bytes 294920
  513.0 3.4 collective-permute-start.41
  516.4 6.5 collective-permute-start.42
  523.0 3.4 collective-permute-start.43
  527.9 5.0 collective-permute-start.45
  532.9 5.0 collective-permute-start.46
  537.9 2.2 collective-permute-start.47
  540.1 4.8 collective-permute-start.48
  544.9 3.4 collective-permute-start.49
  554.5 8.6 %collective-permute-start.54 = (f32[16,1536]{1,0:T(8,128)S(1)}, f32[16,1536]{1,0:T(8,128)S(1)}, u32[]{:S(2)}, u32[]{:S(2)}) collective-permute-start(f32[16,1536]{1,0:T(8,128)S(1)} %get-tuple-element.46), channel_id=1, source_target_pairs={{0,23},{1,24},{2,25},{3,26},{4,27},{5,28},{6,29},{7,30},{8,31},{9,... | collective-permute-start | bytes 294920
  567.1 3.6 collective-permute-start.58
  574.9 2.6 collective-permute-start.62
  579.1 3.3 collective-permute-start.1
  582.5 7.9 collective-permute-start.10
  591.8 6.4 collective-permute-start.12
  598.3 2.1 collective-permute-start.13
  600.4 6.4 collective-permute-start.14
  609.6 5.1 collective-permute-start.17
  614.8 3.1 collective-permute-start.18
  619.6 2.2 collective-permute-start.2
  623.8 2.4 collective-permute-start.21
  626.2 2.4 collective-permute-start.22
  634.4 2.2 collective-permute-start.26
  640.4 2.4 collective-permute-start.29
  642.8 13.0 %collective-permute-start.3 = (f32[16,1536]{1,0:T(8,128)S(1)}, f32[16,1536]{1,0:T(8,128)}, u32[]{:S(2)}, u32[]{:S(2)}) collective-permute-start(f32[16,1536]{1,0:T(8,128)S(1)} %get-tuple-element.45), channel_id=1, source_target_pairs={{0,4},{1,5},{2,6},{3,7},{4,8},{5,9},{6,10},{7,11},{8,12},{9,13},{1... | collective-permute-start | bytes 294920
  660.1 31.7 %concatenate.1 = f32[524,1536]{1,0:T(8,128)S(1)} concatenate(f32[12,1536]{1,0:T(8,128)} %copy-done.2, f32[16,1536]{1,0:T(8,128)} %copy-done.40, f32[16,1536]{1,0:T(8,128)} %copy-done.38, f32[16,1536]{1,0:T(8,128)} %copy-done.36, f32[16,1536]{1,0:T(8,128)} %copy-done.34, f32[16,1536]{1,0:T(8,128)} %copy-done.32, f32[16,1536]{1,0:T(8,128)} %copy-done.30, f32[16,1536]{1,0:T(8,128)} %copy-done.28, ...), dimensions={0} | concatenate | bytes 6438912
  696.0 6.4 collective-permute-start.8
  702.5 3.8 collective-permute-start.9
  708.3 30.0 %concatenate = f32[524,1536]{1,0:T(8,128)S(1)} concatenate(f32[12,1536]{1,0:T(8,128)S(1)} %collective-permute-done.31, f32[16,1536]{1,0:T(8,128)} %collective-permute-done.30, f32[16,1536]{1,0:T(8,128)} %collective-permute-done.29, f32[16,1536]{1,0:T(8,128)} %collective-permute-done.28, f32[16,1536]{1,0:T(8,128)} %collective-permute-done.27, f32[16,1536]{1,0:T(8,128)} %collective-permute-done.26, ...), dimensions={0} | concatenate | bytes 6438912
  739.0 56.1 %all-reduce.8.cloned.1.call-done = f32[40,1536]{1,0:T(8,128)} async-done(((f32[40,1536]{1,0:T(8,128)}), f32[40,1536]{1,0:T(8,128)}) %all-reduce.8.cloned.1.call-update) | async-done | bytes 245776
  (220 shorter events, 74.3 us)
Async XLA Ops:
  7.2 787.9 %all-reduce.8.cloned.1.call-start = ((), (), s32[]{:S(2)}) async-start(), calls=%async_computation | async-start | bytes 491520
  493.6 19.3 %collective-permute-start.36 = (f32[16,1536]{1,0:T(8,128)S(1)}, f32[16,1536]{1,0:T(8,128)S(1)}, u32[]{:S(2)}, u32[]{:S(2)}) collective-permute-start(f32[16,1536]{1,0:T(8,128)S(1)} %get-tuple-element.46), channel_id=1, source_target_pairs={{0,5},{1,6},{2,7},{3,8},{4,9},{5,10},{6,11},{7,12},{8,13},{9,14},{... | collective-permute-start | bytes 294920
  494.9 21.5 %collective-permute-start.37 = (f32[16,1536]{1,0:T(8,128)S(1)}, f32[16,1536]{1,0:T(8,128)S(1)}, u32[]{:S(2)}, u32[]{:S(2)}) collective-permute-start(f32[16,1536]{1,0:T(8,128)S(1)} %get-tuple-element.46), channel_id=1, source_target_pairs={{0,6},{1,7},{2,8},{3,9},{4,10},{5,11},{6,12},{7,13},{8,14},{9,15},... | collective-permute-start | bytes 294920
  496.3 26.7 %collective-permute-start.38 = (f32[16,1536]{1,0:T(8,128)S(1)}, f32[16,1536]{1,0:T(8,128)S(1)}, u32[]{:S(2)}, u32[]{:S(2)}) collective-permute-start(f32[16,1536]{1,0:T(8,128)S(1)} %get-tuple-element.46), channel_id=1, source_target_pairs={{0,7},{1,8},{2,9},{3,10},{4,11},{5,12},{6,13},{7,14},{8,15},{9,16}... | collective-permute-start | bytes 294920
  497.6 28.8 %collective-permute-start.39 = (f32[16,1536]{1,0:T(8,128)S(1)}, f32[16,1536]{1,0:T(8,128)S(1)}, u32[]{:S(2)}, u32[]{:S(2)}) collective-permute-start(f32[16,1536]{1,0:T(8,128)S(1)} %get-tuple-element.46), channel_id=1, source_target_pairs={{0,8},{1,9},{2,10},{3,11},{4,12},{5,13},{6,14},{7,15},{8,16},{9,17... | collective-permute-start | bytes 294920
  498.9 29.0 %collective-permute-start.40 = (f32[16,1536]{1,0:T(8,128)S(1)}, f32[16,1536]{1,0:T(8,128)S(1)}, u32[]{:S(2)}, u32[]{:S(2)}) collective-permute-start(f32[16,1536]{1,0:T(8,128)S(1)} %get-tuple-element.46), channel_id=1, source_target_pairs={{0,9},{1,10},{2,11},{3,12},{4,13},{5,14},{6,15},{7,16},{8,17},{9,1... | collective-permute-start | bytes 294920
  513.0 19.9 %collective-permute-start.41 = (f32[16,1536]{1,0:T(8,128)S(1)}, f32[16,1536]{1,0:T(8,128)S(1)}, u32[]{:S(2)}, u32[]{:S(2)}) collective-permute-start(f32[16,1536]{1,0:T(8,128)S(1)} %get-tuple-element.46), channel_id=1, source_target_pairs={{0,10},{1,11},{2,12},{3,13},{4,14},{5,15},{6,16},{7,17},{8,18},{9,... | collective-permute-start | bytes 294920
  516.4 21.5 %collective-permute-start.42 = (f32[16,1536]{1,0:T(8,128)S(1)}, f32[16,1536]{1,0:T(8,128)S(1)}, u32[]{:S(2)}, u32[]{:S(2)}) collective-permute-start(f32[16,1536]{1,0:T(8,128)S(1)} %get-tuple-element.46), channel_id=1, source_target_pairs={{0,11},{1,12},{2,13},{3,14},{4,15},{5,16},{6,17},{7,18},{8,19},{9,... | collective-permute-start | bytes 294920
  523.0 17.1 %collective-permute-start.43 = (f32[16,1536]{1,0:T(8,128)S(1)}, f32[16,1536]{1,0:T(8,128)S(1)}, u32[]{:S(2)}, u32[]{:S(2)}) collective-permute-start(f32[16,1536]{1,0:T(8,128)S(1)} %get-tuple-element.46), channel_id=1, source_target_pairs={{0,12},{1,13},{2,14},{3,15},{4,16},{5,17},{6,18},{7,19},{8,20},{9,... | collective-permute-start | bytes 294920
  526.4 18.5 %collective-permute-start.44 = (f32[16,1536]{1,0:T(8,128)S(1)}, f32[16,1536]{1,0:T(8,128)S(1)}, u32[]{:S(2)}, u32[]{:S(2)}) collective-permute-start(f32[16,1536]{1,0:T(8,128)S(1)} %get-tuple-element.46), channel_id=1, source_target_pairs={{0,13},{1,14},{2,15},{3,16},{4,17},{5,18},{6,19},{7,20},{8,21},{9,... | collective-permute-start | bytes 294920
  527.9 20.5 %collective-permute-start.45 = (f32[16,1536]{1,0:T(8,128)S(1)}, f32[16,1536]{1,0:T(8,128)S(1)}, u32[]{:S(2)}, u32[]{:S(2)}) collective-permute-start(f32[16,1536]{1,0:T(8,128)S(1)} %get-tuple-element.46), channel_id=1, source_target_pairs={{0,14},{1,15},{2,16},{3,17},{4,18},{5,19},{6,20},{7,21},{8,22},{9,... | collective-permute-start | bytes 294920
  532.9 16.8 %collective-permute-start.46 = (f32[16,1536]{1,0:T(8,128)S(1)}, f32[16,1536]{1,0:T(8,128)S(1)}, u32[]{:S(2)}, u32[]{:S(2)}) collective-permute-start(f32[16,1536]{1,0:T(8,128)S(1)} %get-tuple-element.46), channel_id=1, source_target_pairs={{0,15},{1,16},{2,17},{3,18},{4,19},{5,20},{6,21},{7,22},{8,23},{9,... | collective-permute-start | bytes 294920
  548.4 14.7 %collective-permute-start.50 = (f32[16,1536]{1,0:T(8,128)S(1)}, f32[16,1536]{1,0:T(8,128)S(1)}, u32[]{:S(2)}, u32[]{:S(2)}) collective-permute-start(f32[16,1536]{1,0:T(8,128)S(1)} %get-tuple-element.46), channel_id=1, source_target_pairs={{0,19},{1,20},{2,21},{3,22},{4,23},{5,24},{6,25},{7,26},{8,27},{9,... | collective-permute-start | bytes 294920
  549.7 14.7 %collective-permute-start.51 = (f32[16,1536]{1,0:T(8,128)S(1)}, f32[16,1536]{1,0:T(8,128)S(1)}, u32[]{:S(2)}, u32[]{:S(2)}) collective-permute-start(f32[16,1536]{1,0:T(8,128)S(1)} %get-tuple-element.46), channel_id=1, source_target_pairs={{0,20},{1,21},{2,22},{3,23},{4,24},{5,25},{6,26},{7,27},{8,28},{9,... | collective-permute-start | bytes 294920
  554.5 16.2 %collective-permute-start.54 = (f32[16,1536]{1,0:T(8,128)S(1)}, f32[16,1536]{1,0:T(8,128)S(1)}, u32[]{:S(2)}, u32[]{:S(2)}) collective-permute-start(f32[16,1536]{1,0:T(8,128)S(1)} %get-tuple-element.46), channel_id=1, source_target_pairs={{0,23},{1,24},{2,25},{3,26},{4,27},{5,28},{6,29},{7,30},{8,31},{9,... | collective-permute-start | bytes 294920
  573.3 17.2 %collective-permute-start.61 = (f32[16,1536]{1,0:T(8,128)S(1)}, f32[16,1536]{1,0:T(8,128)S(1)}, u32[]{:S(2)}, u32[]{:S(2)}) collective-permute-start(f32[16,1536]{1,0:T(8,128)S(1)} %get-tuple-element.46), channel_id=1, source_target_pairs={{0,30},{1,31},{2,32},{3,33},{4,34},{5,35},{6,36},{7,37},{8,38},{9,... | collective-permute-start | bytes 294920
  574.9 17.0 %collective-permute-start.62 = (f32[16,1536]{1,0:T(8,128)S(1)}, f32[16,1536]{1,0:T(8,128)S(1)}, u32[]{:S(2)}, u32[]{:S(2)}) collective-permute-start(f32[16,1536]{1,0:T(8,128)S(1)} %get-tuple-element.46), channel_id=1, source_target_pairs={{0,31},{1,32},{2,33},{3,34},{4,35},{5,36},{6,37},{7,38},{8,39},{9,... | collective-permute-start | bytes 294920
  577.5 20.8 %collective-permute-start = (f32[16,1536]{1,0:T(8,128)S(1)}, f32[16,1536]{1,0:T(8,128)S(1)}, u32[]{:S(2)}, u32[]{:S(2)}) collective-permute-start(f32[16,1536]{1,0:T(8,128)S(1)} %get-tuple-element.45), channel_id=1, source_target_pairs={{0,1},{1,2},{2,3},{3,4},{4,5},{5,6},{6,7},{7,8},{8,9},{9,10},{10,1... | collective-permute-start | bytes 294920
  579.1 21.3 %collective-permute-start.1 = (f32[16,1536]{1,0:T(8,128)S(1)}, f32[16,1536]{1,0:T(8,128)S(1)}, u32[]{:S(2)}, u32[]{:S(2)}) collective-permute-start(f32[16,1536]{1,0:T(8,128)S(1)} %get-tuple-element.45), channel_id=1, source_target_pairs={{0,2},{1,3},{2,4},{3,5},{4,6},{5,7},{6,8},{7,9},{8,10},{9,11},{10,... | collective-permute-start | bytes 294920
  582.5 24.4 %collective-permute-start.10 = (f32[16,1536]{1,0:T(8,128)S(1)}, f32[16,1536]{1,0:T(8,128)S(1)}, u32[]{:S(2)}, u32[]{:S(2)}) collective-permute-start(f32[16,1536]{1,0:T(8,128)S(1)} %get-tuple-element.45), channel_id=1, source_target_pairs={{0,11},{1,12},{2,13},{3,14},{4,15},{5,16},{6,17},{7,18},{8,19},{9,... | collective-permute-start | bytes 294920
  590.5 17.7 %collective-permute-start.11 = (f32[16,1536]{1,0:T(8,128)S(1)}, f32[16,1536]{1,0:T(8,128)S(1)}, u32[]{:S(2)}, u32[]{:S(2)}) collective-permute-start(f32[16,1536]{1,0:T(8,128)S(1)} %get-tuple-element.45), channel_id=1, source_target_pairs={{0,12},{1,13},{2,14},{3,15},{4,16},{5,17},{6,18},{7,19},{8,20},{9,... | collective-permute-start | bytes 294920
  591.8 17.8 %collective-permute-start.12 = (f32[16,1536]{1,0:T(8,128)S(1)}, f32[16,1536]{1,0:T(8,128)S(1)}, u32[]{:S(2)}, u32[]{:S(2)}) collective-permute-start(f32[16,1536]{1,0:T(8,128)S(1)} %get-tuple-element.45), channel_id=1, source_target_pairs={{0,13},{1,14},{2,15},{3,16},{4,17},{5,18},{6,19},{7,20},{8,21},{9,... | collective-permute-start | bytes 294920
  598.3 16.5 %collective-permute-start.13 = (f32[16,1536]{1,0:T(8,128)S(1)}, f32[16,1536]{1,0:T(8,128)S(1)}, u32[]{:S(2)}, u32[]{:S(2)}) collective-permute-start(f32[16,1536]{1,0:T(8,128)S(1)} %get-tuple-element.45), channel_id=1, source_target_pairs={{0,14},{1,15},{2,16},{3,17},{4,18},{5,19},{6,20},{7,21},{8,22},{9,... | collective-permute-start | bytes 294920
  600.4 17.4 %collective-permute-start.14 = (f32[16,1536]{1,0:T(8,128)S(1)}, f32[16,1536]{1,0:T(8,128)S(1)}, u32[]{:S(2)}, u32[]{:S(2)}) collective-permute-start(f32[16,1536]{1,0:T(8,128)S(1)} %get-tuple-element.45), channel_id=1, source_target_pairs={{0,15},{1,16},{2,17},{3,18},{4,19},{5,20},{6,21},{7,22},{8,23},{9,... | collective-permute-start | bytes 294920
  634.4 21.5 %collective-permute-start.26 = (f32[16,1536]{1,0:T(8,128)S(1)}, f32[16,1536]{1,0:T(8,128)}, u32[]{:S(2)}, u32[]{:S(2)}) collective-permute-start(f32[16,1536]{1,0:T(8,128)S(1)} %get-tuple-element.45), channel_id=1, source_target_pairs={{0,27},{1,28},{2,29},{3,30},{4,31},{5,32},{6,33},{7,34},{8,35},{9,... | collective-permute-start | bytes 294920
  636.6 21.2 %collective-permute-start.27 = (f32[16,1536]{1,0:T(8,128)S(1)}, f32[16,1536]{1,0:T(8,128)}, u32[]{:S(2)}, u32[]{:S(2)}) collective-permute-start(f32[16,1536]{1,0:T(8,128)S(1)} %get-tuple-element.45), channel_id=1, source_target_pairs={{0,28},{1,29},{2,30},{3,31},{4,32},{5,33},{6,34},{7,35},{8,36},{9,... | collective-permute-start | bytes 294920
  638.5 53.3 %collective-permute-start.28 = (f32[16,1536]{1,0:T(8,128)S(1)}, f32[16,1536]{1,0:T(8,128)}, u32[]{:S(2)}, u32[]{:S(2)}) collective-permute-start(f32[16,1536]{1,0:T(8,128)S(1)} %get-tuple-element.45), channel_id=1, source_target_pairs={{0,29},{1,30},{2,31},{3,32},{4,33},{5,34},{6,35},{7,36},{8,37},{9,... | collective-permute-start | bytes 294920
  640.4 53.0 %collective-permute-start.29 = (f32[16,1536]{1,0:T(8,128)S(1)}, f32[16,1536]{1,0:T(8,128)}, u32[]{:S(2)}, u32[]{:S(2)}) collective-permute-start(f32[16,1536]{1,0:T(8,128)S(1)} %get-tuple-element.45), channel_id=1, source_target_pairs={{0,30},{1,31},{2,32},{3,33},{4,34},{5,35},{6,36},{7,37},{8,38},{9,... | collective-permute-start | bytes 294920
  642.8 51.9 %collective-permute-start.3 = (f32[16,1536]{1,0:T(8,128)S(1)}, f32[16,1536]{1,0:T(8,128)}, u32[]{:S(2)}, u32[]{:S(2)}) collective-permute-start(f32[16,1536]{1,0:T(8,128)S(1)} %get-tuple-element.45), channel_id=1, source_target_pairs={{0,4},{1,5},{2,6},{3,7},{4,8},{5,9},{6,10},{7,11},{8,12},{9,13},{1... | collective-permute-start | bytes 294920
  655.8 40.2 %collective-permute-start.30 = (f32[16,1536]{1,0:T(8,128)S(1)}, f32[16,1536]{1,0:T(8,128)}, u32[]{:S(2)}, u32[]{:S(2)}) collective-permute-start(f32[16,1536]{1,0:T(8,128)S(1)} %get-tuple-element.45), channel_id=1, source_target_pairs={{0,31},{1,32},{2,33},{3,34},{4,35},{5,36},{6,37},{7,38},{8,39},{9,... | collective-permute-start | bytes 294920
  657.8 44.7 %collective-permute-start.4 = (f32[16,1536]{1,0:T(8,128)S(1)}, f32[16,1536]{1,0:T(8,128)}, u32[]{:S(2)}, u32[]{:S(2)}) collective-permute-start(f32[16,1536]{1,0:T(8,128)S(1)} %get-tuple-element.45), channel_id=1, source_target_pairs={{0,5},{1,6},{2,7},{3,8},{4,9},{5,10},{6,11},{7,12},{8,13},{9,14},{... | collective-permute-start | bytes 294920
  691.8 15.1 %collective-permute-start.5 = (f32[16,1536]{1,0:T(8,128)S(1)}, f32[16,1536]{1,0:T(8,128)S(1)}, u32[]{:S(2)}, u32[]{:S(2)}) collective-permute-start(f32[16,1536]{1,0:T(8,128)S(1)} %get-tuple-element.45), channel_id=1, source_target_pairs={{0,6},{1,7},{2,8},{3,9},{4,10},{5,11},{6,12},{7,13},{8,14},{9,15},... | collective-permute-start | bytes 294920
  (84 other events, 4026.5 us)
Sparse Core Ops, SparseCore 0:
  660.2 134.8 all-reduce.7

commit v2 on v1

--- a/solution.py
+++ b/solution.py
@@ -34,14 +34,23 @@
 
 def kernel(
     len_ref, q_ref, k_ref, v_ref, res_ref, go_ref, wo_hbm, wp_hbm, ng_ref, taps_ref, cb_ref, cg_ref,
-    bo_ref, gr_ref, gq_ref, gk_ref, gv_ref, gp_ref, gw_ref, small_ref,
+    bo_ref, gr_ref, gq_ref, gk_ref, gv_ref, gow_ref, gpw_ref, gker_ref, gvec_ref,
     wo, wp, snd, rcv, kaug, qaug, vta, vaug, pt, inv, obuf, att_t, att, mixed, n1, r1, cin, cp, csum,
     gact, gm, act, gc, gcl, gpad, vacc, lh, rh, dsnd, do, doaug, qz, dz, kt, dst, snd2, rcv2,
-    w_sem, s_q, r_q, s_o, r_o, s_d, r_d, s_g, r_g, s_h, r_h,
+    ng, cg, small_t, rows_t, pterm, p1, pa, pb, p3, px, p4, oterm, o1, oa, ob, o3, ox, o4, wide,
+    w_sem, s_q, r_q, s_o, r_o, s_d, r_d, s_g, r_g, s_h, r_h, s_p, r_p, s_w, r_w,
 ):
     me = lax.axis_index("ctx")
     dp = lax.axis_index("dp")
     length = len_ref[0]
+    core = lax.rem(dp, 2)
+    y = lax.rem(lax.div(dp, 2), 2)
+    z = lax.div(dp, 4)
+    z_up, z_down, z_far = lax.rem(z + 1, 4), lax.rem(z + 3, 4), lax.rem(z + 2, 4)
+    sibling = (dp + 1 - 2 * core, me)
+    across = (dp + 2 - 4 * y, me)
+    upper = (4 * z_up + 2 * y + core, me)
+    lower = (4 * z_down + 2 * y + core, me)
 
     def at(offset):
         return lax.rem(me + (offset + N), N)
@@ -54,6 +63,8 @@
     barrier = pltpu.get_barrier_semaphore()
     for o in range(1, N):
         pl.semaphore_signal(barrier, inc=1, device_id=(dp, at(o)), device_id_type=MESH)
+    for peer in (sibling, across, upper, lower):
+        pl.semaphore_signal(barrier, inc=1, device_id=peer, device_id_type=MESH)
 
     def exchange(source, target, send_sem, recv_sem, h):
         def copy(o):
@@ -96,6 +107,117 @@
     ex_o = [exchange(obuf, att_t, s_o, r_o, h) for h in range(3)]
     ex_d = [exchange(dsnd, do, s_d, r_d, h) for h in range(3)]
     ex_g = [exchange(snd2, rcv2, s_g, r_g, h) for h in range(3)]
+
+    def reducer(term, first, far, near, pair, split, last, send_sem, recv_sem):
+        def to(source, target, k, device):
+            return pltpu.make_async_remote_copy(
+                src_ref=source,
+                dst_ref=target,
+                send_sem=send_sem.at[k],
+                recv_sem=recv_sem.at[k],
+                device_id=device,
+                device_id_type=MESH,
+            )
+
+        def cores(i):
+            return to(term.at[1 - core, i], first.at[i], i, sibling)
+
+        far_copies = (
+            to(term.at[core, 2 * z_far], far.at[0], 8, upper),
+            to(term.at[core, 2 * z_far + 1], far.at[1], 9, lower),
+        )
+        plain_copies = (
+            to(term.at[core, 2 * z_up + 1], near.at[0, 1], 10, upper),
+            to(term.at[core, 2 * z_down], near.at[1, 0], 11, lower),
+        )
+        joint_copies = (
+            to(term.at[core, 2 * z_up], near.at[0, 0], 12, upper),
+            to(term.at[core, 2 * z_down + 1], near.at[1, 1], 13, lower),
+        )
+        y_copy = to(term.at[core, 2 * z + 1 - y], pair, 14, across)
+
+        def ctx_copy(o):
+            return to(split.at[at(o)], last.at[me], 15 + o, (dp, at(o)))
+
+        def ctx_arrival(o):
+            return to(split.at[at(o)], last.at[at(-o)], 15 + o, (dp, at(-o)))
+
+        def start_z():
+            def add(i, carry):
+                cores(i).wait_recv()
+                term[core, i] = term[core, i] + first[i]
+                return carry
+
+            lax.fori_loop(0, 8, add, 0)
+            for copy in far_copies + plain_copies:
+                copy.start()
+
+        def join_z():
+            for copy, i in zip(far_copies, (2 * z_up, 2 * z_down + 1)):
+                copy.wait_recv()
+                term[core, i] = term[core, i] + far[0 if copy is far_copies[0] else 1]
+            for copy in joint_copies:
+                copy.start()
+
+        def start_y():
+            for copy in plain_copies + joint_copies:
+                copy.wait_recv()
+            for a in (0, 1):
+                total = near[0, a].astype(F32) + near[1, a].astype(F32)
+                term[core, 2 * z + a] = (term[core, 2 * z + a].astype(F32) + total).astype(BF)
+            y_copy.start()
+
+        def start_ctx():
+            y_copy.wait_recv()
+            width = term.shape[3]
+            wide[96:, :width] = jnp.zeros((8, width), F32)
+            wide[:96, :width] = term[core, 2 * z + y].astype(F32) + pair[...].astype(F32)
+            for j in range(N):
+                split[j] = wide[12 * j : 12 * j + 16, :width].astype(BF)
+            for o in range(1, N):
+                ctx_copy(o).start()
+            last[me] = split[me]
+
+        def finish():
+            for o in range(1, N):
+                ctx_arrival(o).wait_recv()
+            total = last[0].astype(F32)
+            for j in range(1, N):
+                total = total + last[j].astype(F32)
+            return total
+
+        def drain():
+            for i in range(8):
+                cores(i).wait_send()
+            for copy in far_copies + plain_copies + joint_copies + (y_copy,):
+                copy.wait_send()
+            for o in range(1, N):
+                ctx_copy(o).wait_send()
+
+        return cores, start_z, join_z, start_y, start_ctx, finish, drain
+
+    point = reducer(pterm, p1, pa, pb, p3, px, p4, s_p, r_p)
+    out = reducer(oterm, o1, oa, ob, o3, ox, o4, s_w, r_w)
+
+    def weight_term(rows, others, term, send):
+        for c in range(NB):
+            rows_t[c * 128 : (c + 1) * 128, :] = rows[:, c * 128 : (c + 1) * 128].T
+
+        def block(i, carry):
+            left = rows_t[pl.ds(pl.multiple_of(i * 192, 192), 192), :]
+            for n in range(3):
+                cols = slice(n * 512, (n + 1) * 512)
+                part = dot(left, others[:, cols]).astype(BF)
+                term[0, i, :, cols] = part[:96]
+                term[1, i, :, cols] = part[96:]
+            if term.shape[3] > D:
+                for a in range(2):
+                    at_rows = pl.ds(pl.multiple_of(i * 192 + a * 96, 96), 96)
+                    term[a, i, :, D:] = small_t[at_rows, :]
+            send(i).start()
+            return carry
+
+        lax.fori_loop(0, 8, block, 0)
 
     for h in range(3):
         for b in range(4):
@@ -108,8 +230,12 @@
                 snd[h, 2 * b, a * HD : (a + 1) * HD, :] = block[:HD]
                 snd[h, 2 * b + 1, a * HD : (a + 1) * HD, :] = block[HD:]
         if h == 0:
-            pl.semaphore_wait(barrier, N - 1)
+            pl.semaphore_wait(barrier, N + 3)
         ex_q[h][0]()
+
+    for c in range(NB):
+        ng[:, c * 128 : (c + 1) * 128] = ng_ref[c : c + 1, :]
+        cg[:, c * 128 : (c + 1) * 128] = cg_ref[c : c + 1, :]
 
     own_valid = me * F + iota((F, 1), 0) < length
     gm[...] = jnp.where(own_valid, go_ref[...], jnp.zeros_like(go_ref))
@@ -188,7 +314,7 @@
         n1[rows, :] = n
         r1[rows, :] = r
         valid = me * F + i * 16 + iota((16, 1), 0) < length
-        low = jnp.where(valid, n * ng_ref[...], 0.0).astype(BF)
+        low = jnp.where(valid, n * ng[...], 0.0).astype(BF)
         cin[rows, :] = low
         wide = low.astype(F32)
         for c in range(NB):
@@ -232,7 +358,7 @@
 
     def convolve(c, carry):
         cols = pl.ds(pl.multiple_of(c * 128, 128), 128)
-        total = jnp.broadcast_to(cb_ref[:, cols], (F, 128))
+        total = jnp.broadcast_to(cb_ref[pl.ds(c, 1), :], (F, 128))
         for t in range(KERN):
             total = total + cp[c, t + 1 : t + 1 + F, :] * taps_ref[t : t + 1, cols]
         csum[:, cols] = total
@@ -251,12 +377,12 @@
         x = x - mean_of(x)
         r = lax.rsqrt(mean_of(x * x) + EPSILON)
         n = x * r
-        y = n * cg_ref[...]
+        y = n * cg[...]
         g = jax.nn.sigmoid(y)
         act[rows, :] = (y * g).astype(BF)
         back = gact[rows, :] * g * (1.0 + y * (1.0 - g))
         vacc[2] += fold(back * n)
-        u = back * cg_ref[...]
+        u = back * cg[...]
         grad = r * (u - mean_of(u) - n * mean_of(u * n))
         vacc[0] += fold(grad)
         low = grad.astype(BF)
@@ -281,12 +407,7 @@
 
     lax.fori_loop(0, D // 256, block_cols, 0)
 
-    def point_rows(c, carry):
-        cols = pl.ds(pl.multiple_of(c * 128, 128), 128)
-        gp_ref[cols, :] = dot(gm[:, cols].T, act[...])
-        return carry
-
-    lax.fori_loop(0, NB, point_rows, 0)
+    weight_term(gm, act, pterm, point[0])
 
     for copy in halo2:
         copy.wait()
@@ -301,13 +422,14 @@
         return carry
 
     lax.fori_loop(0, NB, convolve_back, 0)
+    point[1]()
 
     def first_norm_back(i, carry):
         rows = pl.ds(pl.multiple_of(i * 16, 16), 16)
         x = csum[rows, :]
         n = n1[rows, :]
         vacc[1] += fold(x * n)
-        u = x * ng_ref[...]
+        u = x * ng[...]
         grad = r1[rows, :] * (u - mean_of(u) - n * mean_of(u * n))
         gr_ref[rows, :] = (gm[rows, :].astype(F32) + grad).astype(BF)
         return carry
@@ -327,24 +449,23 @@
         lax.fori_loop(0, 2, attended_rows, 0)
         ex_d[h][0]()
 
-    def out_rows(c, carry):
-        cols = pl.ds(pl.multiple_of(c * 128, 128), 128)
-        gw_ref[cols, :] = dot(gr_ref[:, cols].T, att[...])
-        return carry
-
-    lax.fori_loop(0, NB, out_rows, 0)
+    small = csum
 
     def tap_rows(c, carry):
         cols = pl.ds(pl.multiple_of(c * 128, 128), 128)
         grad = gc[c]
         for t in range(KERN):
-            small_ref[t : t + 1, cols] = jnp.sum(cp[c, t + 1 : t + 1 + F, :] * grad, axis=0, keepdims=True)
+            small[t : t + 1, cols] = jnp.sum(cp[c, t + 1 : t + 1 + F, :] * grad, axis=0, keepdims=True)
         return carry
 
     lax.fori_loop(0, NB, tap_rows, 0)
     for i in range(3):
-        small_ref[KERN + i : KERN + i + 1, :] = jnp.sum(vacc[i], axis=0, keepdims=True)
-    small_ref[KERN + 3 :, :] = jnp.zeros((40 - KERN - 3, D), F32)
+        small[KERN + i : KERN + i + 1, :] = jnp.sum(vacc[i], axis=0, keepdims=True)
+    small[KERN + 3 :, :] = jnp.zeros((128 - KERN - 3, D), F32)
+    for c in range(NB):
+        small_t[c * 128 : (c + 1) * 128, :] = small[:, c * 128 : (c + 1) * 128].T.astype(BF)
+    weight_term(gr_ref, att, oterm, out[0])
+    point[2]()
 
     for h in range(3):
         ex_d[h][1]()
@@ -382,6 +503,14 @@
 
         lax.fori_loop(0, N, back_keys, 0)
         ex_g[h][0]()
+        if h == 0:
+            point[3]()
+            out[1]()
+        elif h == 1:
+            point[4]()
+            out[2]()
+        else:
+            out[3]()
 
     for h in range(3):
         ex_g[h][1]()
@@ -392,6 +521,20 @@
                 pair = jnp.concatenate([rcv2[h, 2 * b, part], rcv2[h, 2 * b + 1, part]], axis=0)
                 ref[:, cols] = pair.T
 
+        if h == 0:
+            out[4]()
+
+    point_total = point[5]()
+    out_total = out[5]()
+    for c in range(NB):
+        cols = slice(c * 128, (c + 1) * 128)
+        gpw_ref[cols, :] = point_total[:, cols].T[:, :12]
+        gow_ref[cols, :] = out_total[:, cols].T[:, :12]
+    tail = out_total[:, D:].T
+    gker_ref[...] = tail[:KERN, :12]
+    gvec_ref[...] = tail[KERN : KERN + 3, :12]
+    point[6]()
+    out[6]()
     for group in (ex_q, ex_o, ex_d, ex_g):
         for h in range(3):
             group[h][2]()
@@ -441,26 +584,39 @@
         pltpu.VMEM((S, S), BF),
         pltpu.VMEM((3, N, 3 * HD, F), BF),
         pltpu.VMEM((3, N, 3 * HD, F), BF),
+        pltpu.VMEM((1, D), F32),
+        pltpu.VMEM((1, D), F32),
+        pltpu.VMEM((D, 128), BF),
+        pltpu.VMEM((D, F), BF),
+        *[
+            pltpu.VMEM(shape + (width,), BF)
+            for width in (D, D + 128)
+            for shape in ((2, 8, 96), (8, 96), (2, 96), (2, 2, 96), (96,), (N, 16), (N, 16))
+        ],
+        pltpu.VMEM((104, D + 128), F32),
         dma((2,)),
         dma((3, N)), dma((3, N)),
         dma((3, N)), dma((3, N)),
         dma((3, N)), dma((3, N)),
         dma((3, N)), dma((3, N)),
         dma((4,)), dma((4,)),
+        dma((23,)), dma((23,)),
+        dma((23,)), dma((23,)),
     ]
     return pl.pallas_call(
         kernel,
         out_shape=[rows] * 5
         + [
-            jax.ShapeDtypeStruct((D, D), F32),
-            jax.ShapeDtypeStruct((D, D), F32),
-            jax.ShapeDtypeStruct((40, D), F32),
+            jax.ShapeDtypeStruct((D, 12), F32),
+            jax.ShapeDtypeStruct((D, 12), F32),
+            jax.ShapeDtypeStruct((KERN, 12), F32),
+            jax.ShapeDtypeStruct((3, 12), F32),
         ],
         in_specs=[smem] + [vmem] * 5 + [hbm] * 2 + [vmem] * 4,
-        out_specs=[vmem] * 8,
+        out_specs=[vmem] * 9,
         scratch_shapes=scratch,
         compiler_params=pltpu.CompilerParams(
-            collective_id=0, has_side_effects=True, vmem_limit_bytes=60 * 1024 * 1024
+            collective_id=0, has_side_effects=True, vmem_limit_bytes=62 * 1024 * 1024
         ),
     )(lengths, q, k, v, res, go, wo, wp, ng, taps, cb, cg)
 
@@ -471,15 +627,10 @@
 ):
     outs = fused(
         lengths, query_rows[0], key_rows[0], value_rows[0], residual_in[0], grad_out[0],
-        out_weight, point_weight, norm_gain[None], conv_kernel, conv_bias[None], conv_gain[None],
+        out_weight, point_weight, norm_gain.reshape(NB, 128), conv_kernel,
+        conv_bias.reshape(NB, 128), conv_gain.reshape(NB, 128),
     )
-    rows = [x[None] for x in outs[:5]]
-    point_term, out_term, small = outs[5:]
-    axes = ("dp", "ctx")
-    out_grad = lax.psum_scatter(out_term, axes, scatter_dimension=0, tiled=True).T
-    point_grad = lax.psum_scatter(point_term, axes, scatter_dimension=0, tiled=True).T
-    small = lax.psum_scatter(small, axes, scatter_dimension=1, tiled=True)
-    return (*rows, out_grad, point_grad, small[:KERN], small[KERN : KERN + 3])
+    return (*[x[None] for x in outs[:5]], *outs[5:])
 
 
 def solution(mesh):

time: 820 us -> 132 us (0.16)
  blocking collectives: 385 us -> 0 us
  starting transfers between devices: 187 us -> 0 us
  local copies, waits for them, and re-layouts: 80.2 us -> 13.9 us
  waiting for transfers between devices: 56.3 us -> 0 us
  Pallas kernels: 88.2 us -> 115 us
  between operations: 16.3 us -> 1.32 us
    unnamed x1 -> x0, blocking collectives: 385 us -> none
    unnamed x65 -> x0, starting transfers between devices: 187 us -> none
    unnamed x112 -> x13, local copies, waits for them, and re-layouts: 72.8 us -> 13.9 us
    unnamed x66 -> x0, waiting for transfers between devices: 56.3 us -> none
    pallas_call x1, Pallas kernels: 88.2 us -> 115 us  [fused(): pl.pallas_call(kernel, out_shape=[rows] * 5 + [jax.ShapeDtypeStruct((D, 1...]
  transfers between devices with their start and end apart: 65 -> 0, of which waited for: 1 -> 0; matrix products, arithmetic and copies ran while one was open for 8% -> 0% of each run, Pallas kernels for 0% -> 0%
where the time goes in v2:
time: 132 us; the launch traced here: 130 us
  Pallas kernels  115 us (87%)
  local copies, waits for them, and re-layouts  13.9 us (11%)
  between operations  1.32 us (1%)
    pallas_call x1, Pallas kernels, fused(): pl.pallas_call(kernel, out_shape=[rows] * 5 + [jax.ShapeDtypeStruct((D, 1...  115 us
    unnamed x13, local copies, waits for them, and re-layouts  13.9 us

profile of v2, /device:TPU:0, one launch (start us, length us, event | category | flops | bytes accessed | tf_op | source)
XLA Modules:
  0.0 130.1 jit_solution(183903341213157082)
XLA Ops:
  1.3 114.8 %shard_map.187 = (bf16[128,1536]{1,0:T(8,128)(2,1)}, bf16[128,1536]{1,0:T(8,128)(2,1)}, bf16[128,1536]{1,0:T(8,128)(2,1)}, bf16[128,1536]{1,0:T(8,128)(2,1)}, bf...) custom-call(s32[1]{0:T(128)S(6)} %copy.30.len_ref, ...), custom_call_target="tpu_custom_call" | custom-call | tf_op jit(solution)/shard_map/pallas_call | solution.py:606
  116.1 0.0 copy-start
  116.1 0.0 copy-start.1
  116.2 1.4 %copy.23 = f32[31,12]{0,1:T(8,128)} copy(f32[31,12]{1,0:T(8,128)} %get-tuple-element.34) | data formatting | bytes 2976
  117.6 2.0 %copy.21 = f32[1536,12]{0,1:T(8,128)} copy(f32[1536,12]{1,0:T(8,128)} %get-tuple-element.32) | data formatting | bytes 147456
  119.6 2.0 %copy.22 = f32[1536,12]{0,1:T(8,128)} copy(f32[1536,12]{1,0:T(8,128)} %get-tuple-element.33) | data formatting | bytes 147456
  121.7 1.8 %copy.31 = bf16[1,128,1536]{2,1,0:T(8,128)(2,1)} copy(bf16[1,128,1536]{2,1,0:T(8,128)(2,1)} %bitcast.22) | data formatting | bytes 786432
  123.4 1.8 %copy.32 = bf16[1,128,1536]{2,1,0:T(8,128)(2,1)} copy(bf16[1,128,1536]{2,1,0:T(8,128)(2,1)} %bitcast.21) | data formatting | bytes 786432
  125.2 1.8 %copy.33 = bf16[1,128,1536]{2,1,0:T(8,128)(2,1)} copy(bf16[1,128,1536]{2,1,0:T(8,128)(2,1)} %bitcast.20) | data formatting | bytes 786432
  127.0 1.8 %copy.34 = bf16[1,128,1536]{2,1,0:T(8,128)(2,1)} copy(bf16[1,128,1536]{2,1,0:T(8,128)(2,1)} %bitcast.19) | data formatting | bytes 786432
  128.7 0.0 copy-done
  128.7 0.7 copy.35
  129.5 0.0 copy-done.1
  129.5 0.6 copy.36
Async XLA Ops:
  116.1 12.6 %copy-start = (bf16[128,1536]{1,0:T(8,128)(2,1)S(1)}, bf16[128,1536]{1,0:T(8,128)(2,1)}, u32[]{:S(2)}) copy-start(bf16[128,1536]{1,0:T(8,128)(2,1)} %get-tuple-element.22) | copy-start | bytes 1179652
  116.1 13.3 %copy-start.1 = (f32[3,12]{1,0:T(4,128)S(1)}, f32[3,12]{1,0:T(4,128)}, u32[]{:S(2)}) copy-start(f32[3,12]{1,0:T(4,128)} %get-tuple-element.53) | copy-start | bytes 436

commit v3 on v2

--- a/solution.py
+++ b/solution.py
@@ -33,12 +33,12 @@
 
 
 def kernel(
-    len_ref, q_ref, k_ref, v_ref, res_ref, go_ref, wo_hbm, wp_hbm, ng_ref, taps_ref, cb_ref, cg_ref,
-    bo_ref, gr_ref, gq_ref, gk_ref, gv_ref, gow_ref, gpw_ref, gker_ref, gvec_ref,
-    wo, wp, snd, rcv, kaug, qaug, vta, vaug, pt, inv, obuf, att_t, att, mixed, n1, r1, cin, cp, csum,
-    gact, gm, act, gc, gcl, gpad, vacc, lh, rh, dsnd, do, doaug, qz, dz, kt, dst, snd2, rcv2,
+    len_ref, q_hbm, k_hbm, v_hbm, res_hbm, go_hbm, wo_hbm, wp_hbm, ng_ref, taps_ref, cb_ref, cg_ref,
+    bo_hbm, gr_hbm, gq_hbm, gk_hbm, gv_hbm, gw_ref, gp_ref,
+    q_ref, k_ref, v_ref, res_ref, go_ref, bo_ref, gr_ref, gq_ref, gk_ref, gv_ref, wo, wp, snd, rcv, kaug, qaug, vta, vaug, pt, inv, obuf, att_t, att, mixed, n1, r1, cin, cp, csum,
+    gact, gm, act, gc, gcl, gpad, vacc, lh, rh, dsnd, do, doaug, qz, dz, kt, dst, sq, rq, skv, rkv,
     ng, cg, small_t, rows_t, pterm, p1, pa, pb, p3, px, p4, oterm, o1, oa, ob, o3, ox, o4, wide,
-    w_sem, s_q, r_q, s_o, r_o, s_d, r_d, s_g, r_g, s_h, r_h, s_p, r_p, s_w, r_w,
+    w_sem, i_sem, e_sem, s_q, r_q, s_o, r_o, s_d, r_d, s_g, r_g, s_k, r_k, s_h, r_h, s_p, r_p, s_w, r_w,
 ):
     me = lax.axis_index("ctx")
     dp = lax.axis_index("dp")
@@ -55,16 +55,24 @@
     def at(offset):
         return lax.rem(me + (offset + N), N)
 
-    wp_copy = pltpu.make_async_copy(wp_hbm, wp, w_sem.at[0])
-    wo_copy = pltpu.make_async_copy(wo_hbm, wo, w_sem.at[1])
-    wp_copy.start()
-    wo_copy.start()
-
     barrier = pltpu.get_barrier_semaphore()
     for o in range(1, N):
         pl.semaphore_signal(barrier, inc=1, device_id=(dp, at(o)), device_id_type=MESH)
     for peer in (sibling, across, upper, lower):
         pl.semaphore_signal(barrier, inc=1, device_id=peer, device_id_type=MESH)
+
+    loads = [
+        pltpu.make_async_copy(source, target, i_sem.at[i])
+        for i, (source, target) in enumerate(
+            ((q_hbm, q_ref), (k_hbm, k_ref), (v_hbm, v_ref), (go_hbm, go_ref), (res_hbm, res_ref))
+        )
+    ]
+    for load in loads:
+        load.start()
+    wp_copy = pltpu.make_async_copy(wp_hbm, wp, w_sem.at[0])
+    wo_copy = pltpu.make_async_copy(wo_hbm, wo, w_sem.at[1])
+    wp_copy.start()
+    wo_copy.start()
 
     def exchange(source, target, send_sem, recv_sem, h):
         def copy(o):
@@ -93,6 +101,22 @@
                 copy(o).start()
             target[h, me] = source[h, me]
 
+        def start_one(j):
+            @pl.when(j != me)
+            def _():
+                o = lax.rem(j - me + N, N)
+                pltpu.make_async_remote_copy(
+                    src_ref=source.at[h, j],
+                    dst_ref=target.at[h, me],
+                    send_sem=send_sem.at[h, o],
+                    recv_sem=recv_sem.at[h, o],
+                    device_id=(dp, j),
+                    device_id_type=MESH,
+                ).start()
+
+        def keep():
+            target[h, me] = source[h, me]
+
         def wait():
             for o in range(1, N):
                 arrival(o).wait_recv()
@@ -101,12 +125,13 @@
             for o in range(1, N):
                 copy(o).wait_send()
 
-        return start, wait, drain
+        return start, wait, drain, start_one, keep
 
     ex_q = [exchange(snd, rcv, s_q, r_q, h) for h in range(3)]
     ex_o = [exchange(obuf, att_t, s_o, r_o, h) for h in range(3)]
     ex_d = [exchange(dsnd, do, s_d, r_d, h) for h in range(3)]
-    ex_g = [exchange(snd2, rcv2, s_g, r_g, h) for h in range(3)]
+    ex_g = [exchange(sq, rq, s_g, r_g, h) for h in range(3)]
+    ex_k = [exchange(skv, rkv, s_k, r_k, h) for h in range(3)]
 
     def reducer(term, first, far, near, pair, split, last, send_sem, recv_sem):
         def to(source, target, k, device):
@@ -219,6 +244,8 @@
 
         lax.fori_loop(0, 8, block, 0)
 
+    for load in loads[:3]:
+        load.wait()
     for h in range(3):
         for b in range(4):
             cols = slice((4 * h + b) * 128, (4 * h + b + 1) * 128)
@@ -237,6 +264,7 @@
         ng[:, c * 128 : (c + 1) * 128] = ng_ref[c : c + 1, :]
         cg[:, c * 128 : (c + 1) * 128] = cg_ref[c : c + 1, :]
 
+    loads[3].wait()
     own_valid = me * F + iota((F, 1), 0) < length
     gm[...] = jnp.where(own_valid, go_ref[...], jnp.zeros_like(go_ref))
     wp_copy.wait()
@@ -280,12 +308,15 @@
             rows = (summed[:HD] * scale).astype(BF)
             for a in range(TILE // F):
                 obuf[h, i * (TILE // F) + a] = rows[:, a * F : (a + 1) * F]
+            for a in range(TILE // F):
+                ex_o[h][3](i * (TILE // F) + a)
             return carry
 
         lax.fori_loop(0, S // TILE, attend, 0)
-        ex_o[h][0]()
+        ex_o[h][4]()
 
     wo_copy.wait()
+    loads[4].wait()
     for h in range(3):
         ex_o[h][1]()
         for b in range(4):
@@ -371,30 +402,27 @@
     def fold(x):
         return x[:8] + x[8:]
 
-    def second_norm(i, carry):
-        rows = pl.ds(pl.multiple_of(i * 16, 16), 16)
+    for i in range(F // 16):
+        rows = slice(i * 16, (i + 1) * 16)
         x = csum[rows, :]
         x = x - mean_of(x)
         r = lax.rsqrt(mean_of(x * x) + EPSILON)
         n = x * r
-        y = n * cg[...]
-        g = jax.nn.sigmoid(y)
-        act[rows, :] = (y * g).astype(BF)
-        back = gact[rows, :] * g * (1.0 + y * (1.0 - g))
+        scaled = n * cg[...]
+        g = jax.nn.sigmoid(scaled)
+        act[rows, :] = (scaled * g).astype(BF)
+        back = gact[rows, :] * g * (1.0 + scaled * (1.0 - g))
         vacc[2] += fold(back * n)
         u = back * cg[...]
         grad = r * (u - mean_of(u) - n * mean_of(u * n))
         vacc[0] += fold(grad)
         low = grad.astype(BF)
         gcl[rows, :] = low
-        wide = low.astype(F32)
+        low_wide = low.astype(F32)
         for c in range(NB):
             cols = slice(c * 128, (c + 1) * 128)
             gc[c, rows, :] = grad[:, cols]
-            gpad[c, pl.ds(pl.multiple_of(16 + i * 16, 16), 16), :] = wide[:, cols]
-        return carry
-
-    lax.fori_loop(0, F // 16, second_norm, 0)
+            gpad[c, 16 + i * 16 : 32 + i * 16, :] = low_wide[:, cols]
 
     halo2 = edges(gcl, 1)
     for copy in halo2:
@@ -406,6 +434,8 @@
         return carry
 
     lax.fori_loop(0, D // 256, block_cols, 0)
+    stores = [pltpu.make_async_copy(bo_ref, bo_hbm, e_sem.at[0])]
+    stores[0].start()
 
     weight_term(gm, act, pterm, point[0])
 
@@ -435,6 +465,8 @@
         return carry
 
     lax.fori_loop(0, F // 16, first_norm_back, 0)
+    stores.append(pltpu.make_async_copy(gr_ref, gr_hbm, e_sem.at[1]))
+    stores[1].start()
 
     for h in range(3):
 
@@ -490,7 +522,9 @@
             dst[:, cols] = grads
             rows = (dot(kt[...], grads) * 0.125).astype(BF)
             for a in range(TILE // F):
-                snd2[h, i * (TILE // F) + a, :HD] = rows[:, a * F : (a + 1) * F]
+                sq[h, i * (TILE // F) + a] = rows[:, a * F : (a + 1) * F]
+            for a in range(TILE // F):
+                ex_g[h][3](i * (TILE // F) + a)
             return carry
 
         lax.fori_loop(0, S // TILE, back_queries, 0)
@@ -498,11 +532,13 @@
         def back_keys(j, carry, h=h):
             rows = pl.ds(pl.multiple_of(j * F, F), F)
             both = dot_nt(dst[rows, :], qz[...]) + dot_nt(pt[h, rows, :], dz[...])
-            snd2[h, j, HD:] = both.T.astype(BF)
+            skv[h, j] = both.T.astype(BF)
+            ex_k[h][3](j)
             return carry
 
         lax.fori_loop(0, N, back_keys, 0)
-        ex_g[h][0]()
+        ex_g[h][4]()
+        ex_k[h][4]()
         if h == 0:
             point[3]()
             out[1]()
@@ -514,30 +550,30 @@
 
     for h in range(3):
         ex_g[h][1]()
+        ex_k[h][1]()
         for b in range(4):
             cols = slice((4 * h + b) * 128, (4 * h + b + 1) * 128)
-            for a, ref in enumerate((gq_ref, gk_ref, gv_ref)):
-                part = slice(a * HD, (a + 1) * HD)
-                pair = jnp.concatenate([rcv2[h, 2 * b, part], rcv2[h, 2 * b + 1, part]], axis=0)
+            for ref, source, part in (
+                (gq_ref, rq, slice(0, HD)), (gk_ref, rkv, slice(0, HD)), (gv_ref, rkv, slice(HD, 2 * HD))
+            ):
+                pair = jnp.concatenate([source[h, 2 * b, part], source[h, 2 * b + 1, part]], axis=0)
                 ref[:, cols] = pair.T
-
+        cols = pl.ds(512 * h, 512)
+        for a, (ref, hbm) in enumerate(((gq_ref, gq_hbm), (gk_ref, gk_hbm), (gv_ref, gv_hbm))):
+            stores.append(pltpu.make_async_copy(ref.at[:, cols], hbm.at[:, cols], e_sem.at[2 + 3 * h + a]))
+            stores[-1].start()
         if h == 0:
             out[4]()
 
-    point_total = point[5]()
-    out_total = out[5]()
-    for c in range(NB):
-        cols = slice(c * 128, (c + 1) * 128)
-        gpw_ref[cols, :] = point_total[:, cols].T[:, :12]
-        gow_ref[cols, :] = out_total[:, cols].T[:, :12]
-    tail = out_total[:, D:].T
-    gker_ref[...] = tail[:KERN, :12]
-    gvec_ref[...] = tail[KERN : KERN + 3, :12]
+    gp_ref[...] = point[5]()
+    gw_ref[...] = out[5]()
     point[6]()
     out[6]()
-    for group in (ex_q, ex_o, ex_d, ex_g):
+    for group in (ex_q, ex_o, ex_d, ex_g, ex_k):
         for h in range(3):
             group[h][2]()
+    for store in stores:
+        store.wait()
 
 
 def fused(lengths, q, k, v, res, go, wo, wp, ng, taps, cb, cg):
@@ -547,6 +583,7 @@
     rows = jax.ShapeDtypeStruct((F, D), BF)
     dma = pltpu.SemaphoreType.DMA
     scratch = [
+        *[pltpu.VMEM((F, D), BF)] * 10,
         pltpu.VMEM((D, D), BF),
         pltpu.VMEM((D, D), BF),
         pltpu.VMEM((3, N, 3 * HD, F), BF),
@@ -582,8 +619,10 @@
         pltpu.VMEM((128, S), BF),
         pltpu.VMEM((HD, S), BF),
         pltpu.VMEM((S, S), BF),
-        pltpu.VMEM((3, N, 3 * HD, F), BF),
-        pltpu.VMEM((3, N, 3 * HD, F), BF),
+        pltpu.VMEM((3, N, HD, F), BF),
+        pltpu.VMEM((3, N, HD, F), BF),
+        pltpu.VMEM((3, N, 2 * HD, F), BF),
+        pltpu.VMEM((3, N, 2 * HD, F), BF),
         pltpu.VMEM((1, D), F32),
         pltpu.VMEM((1, D), F32),
         pltpu.VMEM((D, 128), BF),
@@ -595,6 +634,9 @@
         ],
         pltpu.VMEM((104, D + 128), F32),
         dma((2,)),
+        dma((5,)),
+        dma((11,)),
+        dma((3, N)), dma((3, N)),
         dma((3, N)), dma((3, N)),
         dma((3, N)), dma((3, N)),
         dma((3, N)), dma((3, N)),
@@ -606,19 +648,41 @@
     return pl.pallas_call(
         kernel,
         out_shape=[rows] * 5
-        + [
-            jax.ShapeDtypeStruct((D, 12), F32),
-            jax.ShapeDtypeStruct((D, 12), F32),
-            jax.ShapeDtypeStruct((KERN, 12), F32),
-            jax.ShapeDtypeStruct((3, 12), F32),
-        ],
-        in_specs=[smem] + [vmem] * 5 + [hbm] * 2 + [vmem] * 4,
-        out_specs=[vmem] * 9,
+        + [jax.ShapeDtypeStruct((16, D + 128), F32), jax.ShapeDtypeStruct((16, D), F32)],
+        in_specs=[smem] + [hbm] * 7 + [vmem] * 4,
+        out_specs=[hbm] * 5 + [vmem] * 2,
         scratch_shapes=scratch,
         compiler_params=pltpu.CompilerParams(
             collective_id=0, has_side_effects=True, vmem_limit_bytes=62 * 1024 * 1024
         ),
     )(lengths, q, k, v, res, go, wo, wp, ng, taps, cb, cg)
+
+
+def finish(gw_ref, gp_ref, *refs):
+    rows, (gow_ref, gpw_ref, gker_ref, gvec_ref), sems = (refs[:5], refs[5:10]), refs[10:14], refs[14]
+    copies = [pltpu.make_async_copy(a, b, sems.at[i]) for i, (a, b) in enumerate(zip(*rows))]
+    for copy in copies:
+        copy.start()
+    gow_ref[...] = gw_ref[:12, :D]
+    gpw_ref[...] = gp_ref[:12, :]
+    gker_ref[...] = gw_ref[:12, D : D + KERN]
+    gvec_ref[...] = gw_ref[:, D:].T[KERN : KERN + 3, :12]
+    for copy in copies:
+        copy.wait()
+
+
+def finished(rows, gw, gp):
+    vmem = pl.BlockSpec(memory_space=pltpu.VMEM)
+    hbm = pl.BlockSpec(memory_space=pl.ANY)
+    return pl.pallas_call(
+        finish,
+        out_shape=[jax.ShapeDtypeStruct((F, D), BF)] * 5
+        + [jax.ShapeDtypeStruct(shape, F32) for shape in ((12, D), (12, D), (12, KERN), (3, 12))],
+        in_specs=[vmem] * 2 + [hbm] * 5,
+        out_specs=[hbm] * 5 + [vmem] * 4,
+        scratch_shapes=[pltpu.SemaphoreType.DMA((5,))],
+        compiler_params=pltpu.CompilerParams(vmem_limit_bytes=62 * 1024 * 1024),
+    )(gw, gp, *rows)
 
 
 def local(
@@ -630,7 +694,8 @@
         out_weight, point_weight, norm_gain.reshape(NB, 128), conv_kernel,
         conv_bias.reshape(NB, 128), conv_gain.reshape(NB, 128),
     )
-    return (*[x[None] for x in outs[:5]], *outs[5:])
+    outs = finished(outs[:5], *outs[5:])
+    return (*[x[None] for x in outs[:5]], *[x.T for x in outs[5:8]], outs[8])
 
 
 def solution(mesh):

time: 132 us -> 178 us (1.35)
  Pallas kernels: 115 us -> 174 us
  local copies, waits for them, and re-layouts: 13.9 us -> 0 us
    pallas_call x1 -> x2, Pallas kernels: 115 us -> 174 us  [the longest x1 111 us: fused(): pl.pallas_call(kernel, out_shape=[rows] * 5 + [jax.ShapeDtypeStruct((16,...]
    unnamed x13 -> x0, local copies, waits for them, and re-layouts: 13.9 us -> none
where the time goes in v3:
time: 178 us; the launch traced here: 175 us
  Pallas kernels  174 us (98%)
    pallas_call x1, Pallas kernels, fused(): pl.pallas_call(kernel, out_shape=[rows] * 5 + [jax.ShapeDtypeStruct((16,...  111 us
    pallas_call x1, Pallas kernels, finished(): pl.pallas_call(finish, out_shape=[jax.ShapeDtypeStruct((F, D), BF)] * 5 +...  62.3 us

profile of v3, /device:TPU:0, one launch (start us, length us, event | category | flops | bytes accessed | tf_op | source)
XLA Modules:
  0.0 174.8 jit_solution(7723607950183868311)
XLA Ops:
  1.3 111.2 %shard_map.187 = (bf16[128,1536]{1,0:T(8,128)(2,1)}, bf16[128,1536]{1,0:T(8,128)(2,1)}, bf16[128,1536]{1,0:T(8,128)(2,1)}, bf16[128,1536]{1,0:T(8,128)(2,1)}, bf...) custom-call(s32[1]{0:T(128)S(6)} %copy.21.len_ref, bf16[128,1536]{1,0:T(8,128)(2,1)} %bitcast.16, ...), custom_call_target="tpu_custom_call" | custom-call | tf_op jit(solution)/shard_map/pallas_call | solution.py:648
  112.5 62.3 %shard_map.188 = (bf16[128,1536]{1,0:T(8,128)(2,1)}, bf16[128,1536]{1,0:T(8,128)(2,1)}, bf16[128,1536]{1,0:T(8,128)(2,1)}, bf16[128,1536]{1,0:T(8,128)(2,1)}, bf...) custom-call(f32[16,1664]{1,0:T(8,128)} %get-tuple-element.25.gw_ref,, ...), custom_call_target="tpu_custom_call" | custom-call | tf_op jit(solution)/shard_map/pallas_call | solution.py:677

commit v4 on v3

--- a/solution.py
+++ b/solution.py
@@ -36,29 +36,48 @@
     len_ref, q_hbm, k_hbm, v_hbm, res_hbm, go_hbm, wo_hbm, wp_hbm, ng_ref, taps_ref, cb_ref, cg_ref,
     bo_hbm, gr_hbm, gq_hbm, gk_hbm, gv_hbm, gw_ref, gp_ref,
     q_ref, k_ref, v_ref, res_ref, go_ref, bo_ref, gr_ref, gq_ref, gk_ref, gv_ref, wo, wp, snd, rcv, kaug, qaug, vta, vaug, pt, inv, obuf, att_t, att, mixed, n1, r1, cin, cp, csum,
-    gact, gm, act, gc, gcl, gpad, vacc, lh, rh, dsnd, do, doaug, qz, dz, kt, dst, sq, rq, skv, rkv,
-    ng, cg, small_t, rows_t, pterm, p1, pa, pb, p3, px, p4, oterm, o1, oa, ob, o3, ox, o4, wide,
-    w_sem, i_sem, e_sem, s_q, r_q, s_o, r_o, s_d, r_d, s_g, r_g, s_k, r_k, s_h, r_h, s_p, r_p, s_w, r_w,
+    gact, gm, act, gc, gcl, gpad, vacc, lh, rh, dsnd, do, doaug, qz, dz, kt, rq, rkv,
+    ng, cg, small_t, rows_t, rows_p, *rest,
 ):
     me = lax.axis_index("ctx")
     dp = lax.axis_index("dp")
     length = len_ref[0]
+    sums, rest = [rest[7 * i : 7 * i + 7] for i in range(4)], rest[28:]
+    (
+        wide, w_sem, i_sem, e_sem, s_q, r_q, s_o, r_o, s_d, r_d, s_g, r_g, s_k, r_k, s_h, r_h, s_r, r_r,
+    ) = rest
+    dst = wp.at[pl.ds(0, S), pl.ds(0, S)]
+    sq, skv = snd.at[:, :, pl.ds(0, HD)], snd.at[:, :, pl.ds(HD, 2 * HD)]
     core = lax.rem(dp, 2)
     y = lax.rem(lax.div(dp, 2), 2)
     z = lax.div(dp, 4)
-    z_up, z_down, z_far = lax.rem(z + 1, 4), lax.rem(z + 3, 4), lax.rem(z + 2, 4)
-    sibling = (dp + 1 - 2 * core, me)
-    across = (dp + 2 - 4 * y, me)
-    upper = (4 * z_up + 2 * y + core, me)
-    lower = (4 * z_down + 2 * y + core, me)
-
     def at(offset):
         return lax.rem(me + (offset + N), N)
 
+    x = lax.rem(me, 4)
+    y_low = lax.div(me, 4)
+    sibling = (dp + 1 - 2 * core, me)
+
+    def in_z(offset):
+        return lax.rem(z + (offset + 4), 4)
+
+    def in_x(offset):
+        return lax.rem(x + (offset + 4), 4)
+
+    def z_device(offset):
+        return (4 * in_z(offset) + 2 * y + core, me)
+
+    def x_device(offset):
+        return (dp, 4 * y_low + in_x(offset))
+
+    def y_device(other, offset):
+        return (dp + 2 - 4 * y if other else dp, at(offset))
+
+    peers = [sibling] + [z_device(i) for i in (1, 2, 3)]
+    peers += [y_device(b, o) for b in range(2) for o in range(N) if b or o]
+
     barrier = pltpu.get_barrier_semaphore()
-    for o in range(1, N):
-        pl.semaphore_signal(barrier, inc=1, device_id=(dp, at(o)), device_id_type=MESH)
-    for peer in (sibling, across, upper, lower):
+    for peer in peers:
         pl.semaphore_signal(barrier, inc=1, device_id=peer, device_id_type=MESH)
 
     loads = [
@@ -133,116 +152,208 @@
     ex_g = [exchange(sq, rq, s_g, r_g, h) for h in range(3)]
     ex_k = [exchange(skv, rkv, s_k, r_k, h) for h in range(3)]
 
-    def reducer(term, first, far, near, pair, split, last, send_sem, recv_sem):
-        def to(source, target, k, device):
+    def ring(k, along, device):
+        term, first, far, near = sums[k][:4]
+        here = along(0)
+
+        def to(source, target, i, peer):
             return pltpu.make_async_remote_copy(
                 src_ref=source,
                 dst_ref=target,
-                send_sem=send_sem.at[k],
-                recv_sem=recv_sem.at[k],
-                device_id=device,
+                send_sem=s_r.at[k, i],
+                recv_sem=r_r.at[k, i],
+                device_id=peer,
                 device_id_type=MESH,
             )
 
+        up, down = 2 * along(1), 2 * along(-1)
+        opposite = 2 * along(2)
+        far_copies = (
+            to(term.at[core, opposite], far.at[0], 8, device(1)),
+            to(term.at[core, opposite + 1], far.at[1], 9, device(-1)),
+        )
+        plain_copies = (
+            to(term.at[core, up + 1], near.at[0, 1], 10, device(1)),
+            to(term.at[core, down], near.at[1, 0], 11, device(-1)),
+        )
+        joint_copies = (
+            to(term.at[core, up], near.at[0, 0], 12, device(1)),
+            to(term.at[core, down + 1], near.at[1, 1], 13, device(-1)),
+        )
+
         def cores(i):
             return to(term.at[1 - core, i], first.at[i], i, sibling)
 
-        far_copies = (
-            to(term.at[core, 2 * z_far], far.at[0], 8, upper),
-            to(term.at[core, 2 * z_far + 1], far.at[1], 9, lower),
-        )
-        plain_copies = (
-            to(term.at[core, 2 * z_up + 1], near.at[0, 1], 10, upper),
-            to(term.at[core, 2 * z_down], near.at[1, 0], 11, lower),
-        )
-        joint_copies = (
-            to(term.at[core, 2 * z_up], near.at[0, 0], 12, upper),
-            to(term.at[core, 2 * z_down + 1], near.at[1, 1], 13, lower),
-        )
-        y_copy = to(term.at[core, 2 * z + 1 - y], pair, 14, across)
-
-        def ctx_copy(o):
-            return to(split.at[at(o)], last.at[me], 15 + o, (dp, at(o)))
-
-        def ctx_arrival(o):
-            return to(split.at[at(o)], last.at[at(-o)], 15 + o, (dp, at(-o)))
-
-        def start_z():
-            def add(i, carry):
+        def start():
+            order = (opposite, opposite + 1, up + 1, down, up, down + 1, 2 * here, 2 * here + 1)
+            for i, copy in zip(order, far_copies + plain_copies + (None,) * 4):
                 cores(i).wait_recv()
                 term[core, i] = term[core, i] + first[i]
-                return carry
-
-            lax.fori_loop(0, 8, add, 0)
-            for copy in far_copies + plain_copies:
-                copy.start()
-
-        def join_z():
-            for copy, i in zip(far_copies, (2 * z_up, 2 * z_down + 1)):
+                if copy is not None:
+                    copy.start()
+
+        def join():
+            for a, (copy, i) in enumerate(zip(far_copies, (up, down + 1))):
                 copy.wait_recv()
-                term[core, i] = term[core, i] + far[0 if copy is far_copies[0] else 1]
-            for copy in joint_copies:
-                copy.start()
-
-        def start_y():
+                term[core, i] = term[core, i] + far[a]
+                joint_copies[a].start()
+
+        def total():
             for copy in plain_copies + joint_copies:
                 copy.wait_recv()
-            for a in (0, 1):
-                total = near[0, a].astype(F32) + near[1, a].astype(F32)
-                term[core, 2 * z + a] = (term[core, 2 * z + a].astype(F32) + total).astype(BF)
-            y_copy.start()
-
-        def start_ctx():
-            y_copy.wait_recv()
-            width = term.shape[3]
-            wide[96:, :width] = jnp.zeros((8, width), F32)
-            wide[:96, :width] = term[core, 2 * z + y].astype(F32) + pair[...].astype(F32)
-            for j in range(N):
-                split[j] = wide[12 * j : 12 * j + 16, :width].astype(BF)
-            for o in range(1, N):
-                ctx_copy(o).start()
-            last[me] = split[me]
-
-        def finish():
-            for o in range(1, N):
-                ctx_arrival(o).wait_recv()
-            total = last[0].astype(F32)
-            for j in range(1, N):
-                total = total + last[j].astype(F32)
-            return total
+            parts = []
+            for a in range(2):
+                part = term[core, 2 * here + a].astype(F32) + near[0, a].astype(F32)
+                parts.append(part + near[1, a].astype(F32))
+            return parts
 
         def drain():
             for i in range(8):
                 cores(i).wait_send()
-            for copy in far_copies + plain_copies + joint_copies + (y_copy,):
+            for copy in far_copies + plain_copies + joint_copies:
                 copy.wait_send()
-            for o in range(1, N):
-                ctx_copy(o).wait_send()
-
-        return cores, start_z, join_z, start_y, start_ctx, finish, drain
-
-    point = reducer(pterm, p1, pa, pb, p3, px, p4, s_p, r_p)
-    out = reducer(oterm, o1, oa, ob, o3, ox, o4, s_w, r_w)
-
-    def weight_term(rows, others, term, send):
+
+        return to, cores, start, join, total, drain
+
+    def slices(part, split, count):
+        rows, width = part.shape
+        wide[rows : rows + 8, :width] = jnp.zeros((8, width), F32)
+        wide[:rows, :width] = part
+        for j in range(count):
+            split[j] = wide[12 * j : 12 * j + 16, :width].astype(BF)
+
+    def z_reducer(k):
+        to, cores, start, join, total, drain_ring = ring(k, in_z, z_device)
+        split, last = sums[k][5], sums[k][6]
+        others = [(b, o) for b in range(2) for o in range(N) if b or o]
+
+        def sent(b, o):
+            side = 1 - y if b else y
+            return to(split.at[side, at(o)], last.at[y, me], 14 + N * b + o, y_device(b, o))
+
+        def arrival(b, o):
+            block = last.at[1 - y if b else y, at(-o)]
+            return to(block, block, 14 + N * b + o, y_device(b, -o))
+
+        def spread():
+            for a, part in enumerate(total()):
+                slices(part, split.at[a], N)
+            for b, o in others:
+                sent(b, o).start()
+            last[y, me] = split[y, me]
+
+        def finish():
+            for b, o in others:
+                arrival(b, o).wait_recv()
+            result = jnp.zeros(last.shape[2:], F32)
+            for b in range(2):
+                for j in range(N):
+                    result = result + last[b, j].astype(F32)
+            return result
+
+        def drain():
+            drain_ring()
+            for b, o in others:
+                sent(b, o).wait_send()
+
+        return cores, start, join, spread, finish, drain
+
+    def x_reducer(k):
+        to, cores, start, join, total, drain_ring = ring(k, in_x, x_device)
+        term = sums[k][0]
+        in_column, split, last = sums[k][4:]
+
+        def column(o):
+            c = in_z(o)
+            rows = pl.ds(pl.multiple_of(48 * lax.rem(c, 2), 16), 48)
+            return to(term.at[core, 2 * x + lax.div(c, 2), rows], in_column.at[z], 13 + o, z_device(o))
+
+        def column_arrival(o):
+            block = in_column.at[in_z(-o)]
+            return to(block, block, 13 + o, z_device(-o))
+
+        def quad(b):
+            low, high = (1 - y_low if b // 2 else y_low), (1 - y if b % 2 else y)
+            return 2 * low + high, y_device(b % 2, 4 * (b // 2))
+
+        def sent(b):
+            j, peer = quad(b)
+            return to(split.at[j], last.at[2 * y_low + y], 16 + b, peer)
+
+        def arrival(b):
+            j, peer = quad(b)
+            return to(last.at[j], last.at[j], 16 + b, peer)
+
+        def spread_z():
+            for a, part in enumerate(total()):
+                term[core, 2 * x + a] = part.astype(BF)
+            for o in (1, 2, 3):
+                column(o).start()
+
+        def spread():
+            own = pl.ds(pl.multiple_of(48 * lax.rem(z, 2), 16), 48)
+            part = term[core, 2 * x + lax.div(z, 2), own, :].astype(F32)
+            for o in (1, 2, 3):
+                column_arrival(o).wait_recv()
+                part = part + in_column[in_z(-o)].astype(F32)
+            slices(part, split, 4)
+            for b in (1, 2, 3):
+                sent(b).start()
+            last[2 * y_low + y] = split[2 * y_low + y]
+
+        def finish():
+            for b in (1, 2, 3):
+                arrival(b).wait_recv()
+            result = last[0].astype(F32)
+            for j in (1, 2, 3):
+                result = result + last[j].astype(F32)
+            return result
+
+        def drain():
+            drain_ring()
+            for i in (1, 2, 3):
+                column(i).wait_send()
+                sent(i).wait_send()
+
+        return cores, start, join, spread, finish, drain, spread_z
+
+    point_z, point_x = z_reducer(0), x_reducer(1)
+    out_one, out_two = z_reducer(2), z_reducer(3)
+
+    def weight_term(rows, others, begin, width, k, by_z, send):
+        term = sums[k][0]
+
+        def block(i, carry):
+            for a in range(2):
+                if by_z and a:
+                    break
+                base = 192 * i if by_z else 192 * i + 768 * a
+                left = rows[pl.ds(pl.multiple_of(base, 64), 192), :]
+                for n in range(width // 256):
+                    cols = slice(n * 256, (n + 1) * 256)
+                    part = dot(left, others[:, begin + n * 256 : begin + (n + 1) * 256]).astype(BF)
+                    if by_z:
+                        term[0, i, :, cols] = part[:96]
+                        term[1, i, :, cols] = part[96:]
+                    else:
+                        term[a, 2 * i, :, cols] = part[:96]
+                        term[a, 2 * i + 1, :, cols] = part[96:]
+            if term.shape[3] > width:
+                for a in range(2):
+                    at_rows = pl.ds(pl.multiple_of(i * 192 + a * 96, 32), 96)
+                    term[a, i, :, width:] = small_t[at_rows, :]
+            if by_z:
+                send(i).start()
+            else:
+                send(2 * i).start()
+                send(2 * i + 1).start()
+            return carry
+
+        lax.fori_loop(0, 8 if by_z else 4, block, 0)
+
+    def turn(rows):
         for c in range(NB):
             rows_t[c * 128 : (c + 1) * 128, :] = rows[:, c * 128 : (c + 1) * 128].T
-
-        def block(i, carry):
-            left = rows_t[pl.ds(pl.multiple_of(i * 192, 192), 192), :]
-            for n in range(3):
-                cols = slice(n * 512, (n + 1) * 512)
-                part = dot(left, others[:, cols]).astype(BF)
-                term[0, i, :, cols] = part[:96]
-                term[1, i, :, cols] = part[96:]
-            if term.shape[3] > D:
-                for a in range(2):
-                    at_rows = pl.ds(pl.multiple_of(i * 192 + a * 96, 96), 96)
-                    term[a, i, :, D:] = small_t[at_rows, :]
-            send(i).start()
-            return carry
-
-        lax.fori_loop(0, 8, block, 0)
 
     for load in loads[:3]:
         load.wait()
@@ -257,7 +368,7 @@
                 snd[h, 2 * b, a * HD : (a + 1) * HD, :] = block[:HD]
                 snd[h, 2 * b + 1, a * HD : (a + 1) * HD, :] = block[HD:]
         if h == 0:
-            pl.semaphore_wait(barrier, N + 3)
+            pl.semaphore_wait(barrier, len(peers))
         ex_q[h][0]()
 
     for c in range(NB):
@@ -275,6 +386,18 @@
         return carry
 
     lax.fori_loop(0, D // 256, act_grad, 0)
+
+    turn(gm)
+
+    def ordered(b, carry):
+        r = iota((192, 1), 0)
+        d = 384 * lax.div(r, 48) + 48 * lax.rem(lax.div(r, 24), 2) + 192 * lax.rem(lax.div(r, 12), 2)
+        d = d + lax.rem(r, 12) + 96 * lax.div(b, 4) + 12 * lax.rem(b, 4)
+        pick = jnp.where(iota((192, D), 1) == d, 1.0, 0.0).astype(BF)
+        rows_p[pl.ds(pl.multiple_of(192 * b, 64), 192), :] = dot_nt(pick, gm[...]).astype(BF)
+        return carry
+
+    lax.fori_loop(0, 8, ordered, 0)
 
     qaug[HD:, :] = (iota((HD, S), 0) == 0).astype(F32).astype(BF)
     vta[HD:, :] = (iota((16, S), 0) == 0).astype(F32).astype(BF)
@@ -402,7 +525,7 @@
     def fold(x):
         return x[:8] + x[8:]
 
-    for i in range(F // 16):
+    def second_norm(i):
         rows = slice(i * 16, (i + 1) * 16)
         x = csum[rows, :]
         x = x - mean_of(x)
@@ -424,9 +547,14 @@
             gc[c, rows, :] = grad[:, cols]
             gpad[c, 16 + i * 16 : 32 + i * 16, :] = low_wide[:, cols]
 
+    for i in range(F // 16):
+        second_norm(i)
     halo2 = edges(gcl, 1)
     for copy in halo2:
         copy.start()
+
+    weight_term(rows_t, act, 0, 768, 0, True, point_z[0])
+    weight_term(rows_p, act, 768, 768, 1, False, point_x[0])
 
     def block_cols(c, carry):
         cols = pl.ds(pl.multiple_of(c * 256, 256), 256)
@@ -437,7 +565,8 @@
     stores = [pltpu.make_async_copy(bo_ref, bo_hbm, e_sem.at[0])]
     stores[0].start()
 
-    weight_term(gm, act, pterm, point[0])
+    point_z[1]()
+    point_x[1]()
 
     for copy in halo2:
         copy.wait()
@@ -452,7 +581,6 @@
         return carry
 
     lax.fori_loop(0, NB, convolve_back, 0)
-    point[1]()
 
     def first_norm_back(i, carry):
         rows = pl.ds(pl.multiple_of(i * 16, 16), 16)
@@ -481,6 +609,10 @@
         lax.fori_loop(0, 2, attended_rows, 0)
         ex_d[h][0]()
 
+    point_z[2]()
+    point_x[2]()
+    turn(gr_ref)
+    weight_term(rows_t, att, 0, 768, 2, True, out_one[0])
     small = csum
 
     def tap_rows(c, carry):
@@ -496,8 +628,10 @@
     small[KERN + 3 :, :] = jnp.zeros((128 - KERN - 3, D), F32)
     for c in range(NB):
         small_t[c * 128 : (c + 1) * 128, :] = small[:, c * 128 : (c + 1) * 128].T.astype(BF)
-    weight_term(gr_ref, att, oterm, out[0])
-    point[2]()
+    weight_term(rows_t, att, 768, 768, 3, True, out_two[0])
+    out_one[1]()
+    for h in range(3):
+        ex_q[h][2]()
 
     for h in range(3):
         ex_d[h][1]()
@@ -540,13 +674,15 @@
         ex_g[h][4]()
         ex_k[h][4]()
         if h == 0:
-            point[3]()
-            out[1]()
+            out_one[2]()
+            out_two[1]()
+            point_x[6]()
+            point_z[3]()
         elif h == 1:
-            point[4]()
-            out[2]()
+            point_x[3]()
         else:
-            out[3]()
+            out_one[3]()
+            out_two[2]()
 
     for h in range(3):
         ex_g[h][1]()
@@ -562,14 +698,16 @@
         for a, (ref, hbm) in enumerate(((gq_ref, gq_hbm), (gk_ref, gk_hbm), (gv_ref, gv_hbm))):
             stores.append(pltpu.make_async_copy(ref.at[:, cols], hbm.at[:, cols], e_sem.at[2 + 3 * h + a]))
             stores[-1].start()
-        if h == 0:
-            out[4]()
-
-    gp_ref[...] = point[5]()
-    gw_ref[...] = out[5]()
-    point[6]()
-    out[6]()
-    for group in (ex_q, ex_o, ex_d, ex_g, ex_k):
+        if h == 1:
+            out_two[3]()
+
+    gp_ref[:, :768] = point_z[4]()
+    gp_ref[:, 768:] = point_x[4]()
+    gw_ref[:, :768] = out_one[4]()
+    gw_ref[:, 768:] = out_two[4]()
+    for reducer in (point_z, point_x, out_one, out_two):
+        reducer[5]()
+    for group in (ex_o, ex_d, ex_g, ex_k):
         for h in range(3):
             group[h][2]()
     for store in stores:
@@ -618,21 +756,23 @@
         pltpu.VMEM((128, S), BF),
         pltpu.VMEM((128, S), BF),
         pltpu.VMEM((HD, S), BF),
-        pltpu.VMEM((S, S), BF),
         pltpu.VMEM((3, N, HD, F), BF),
-        pltpu.VMEM((3, N, HD, F), BF),
-        pltpu.VMEM((3, N, 2 * HD, F), BF),
         pltpu.VMEM((3, N, 2 * HD, F), BF),
         pltpu.VMEM((1, D), F32),
         pltpu.VMEM((1, D), F32),
         pltpu.VMEM((D, 128), BF),
         pltpu.VMEM((D, F), BF),
+        pltpu.VMEM((D, F), BF),
         *[
             pltpu.VMEM(shape + (width,), BF)
-            for width in (D, D + 128)
-            for shape in ((2, 8, 96), (8, 96), (2, 96), (2, 2, 96), (96,), (N, 16), (N, 16))
+            for width, by_z in ((768, True), (768, False), (768, True), (896, True))
+            for shape in (
+                ((2, 8, 96), (8, 96), (2, 96), (2, 2, 96), (8,), (2, N, 16), (2, N, 16))
+                if by_z
+                else ((2, 8, 96), (8, 96), (2, 96), (2, 2, 96), (4, 48), (4, 16), (4, 16))
+            )
         ],
-        pltpu.VMEM((104, D + 128), F32),
+        pltpu.VMEM((104, 896), F32),
         dma((2,)),
         dma((5,)),
         dma((11,)),
@@ -642,8 +782,7 @@
         dma((3, N)), dma((3, N)),
         dma((3, N)), dma((3, N)),
         dma((4,)), dma((4,)),
-        dma((23,)), dma((23,)),
-        dma((23,)), dma((23,)),
+        dma((4, 30)), dma((4, 30)),
     ]
     return pl.pallas_call(
         kernel,
@@ -659,15 +798,19 @@
 
 
 def finish(gw_ref, gp_ref, *refs):
-    rows, (gow_ref, gpw_ref, gker_ref, gvec_ref), sems = (refs[:5], refs[5:10]), refs[10:14], refs[14]
-    copies = [pltpu.make_async_copy(a, b, sems.at[i]) for i, (a, b) in enumerate(zip(*rows))]
-    for copy in copies:
+    sources, targets, (gow_ref, gpw_ref, gker_ref, gvec_ref), (held, sems) = refs[:5], refs[5:10], refs[10:14], refs[14:]
+    inward = [pltpu.make_async_copy(sources[i], held.at[i], sems.at[0, i]) for i in range(5)]
+    outward = [pltpu.make_async_copy(held.at[i], targets[i], sems.at[1, i]) for i in range(5)]
+    for copy in inward:
         copy.start()
+    for i in range(5):
+        inward[i].wait()
+        outward[i].start()
     gow_ref[...] = gw_ref[:12, :D]
     gpw_ref[...] = gp_ref[:12, :]
     gker_ref[...] = gw_ref[:12, D : D + KERN]
     gvec_ref[...] = gw_ref[:, D:].T[KERN : KERN + 3, :12]
-    for copy in copies:
+    for copy in outward:
         copy.wait()
 
 
@@ -680,7 +823,7 @@
         + [jax.ShapeDtypeStruct(shape, F32) for shape in ((12, D), (12, D), (12, KERN), (3, 12))],
         in_specs=[vmem] * 2 + [hbm] * 5,
         out_specs=[hbm] * 5 + [vmem] * 4,
-        scratch_shapes=[pltpu.SemaphoreType.DMA((5,))],
+        scratch_shapes=[pltpu.VMEM((5, F, D), BF), pltpu.SemaphoreType.DMA((2, 5))],
         compiler_params=pltpu.CompilerParams(vmem_limit_bytes=62 * 1024 * 1024),
     )(gw, gp, *rows)
 

time: 178 us -> 110 us (0.62); the launches traced: 175 us -> 110 us
  Pallas kernels: 174 us -> 109 us
    pallas_call x1, Pallas kernels: 62.3 us -> 3.97 us  [finished(): pl.pallas_call(finish, out_shape=[jax.ShapeDtypeStruct((F, D), BF)] * 5 +...]
    pallas_call x1, Pallas kernels: 111 us -> 105 us  [fused(): pl.pallas_call(kernel, out_shape=[rows] * 5 + [jax.ShapeDtypeStruct((16,...]
where the time goes in v4:
time: 110 us
  Pallas kernels  109 us (99%)
  between operations  1.46 us (1%)
    pallas_call x1, Pallas kernels, fused(): pl.pallas_call(kernel, out_shape=[rows] * 5 + [jax.ShapeDtypeStruct((16,...  105 us
    pallas_call x1, Pallas kernels, finished(): pl.pallas_call(finish, out_shape=[jax.ShapeDtypeStruct((F, D), BF)] * 5 +...  3.97 us

profile of v4, /device:TPU:0, one launch (start us, length us, event | category | flops | bytes accessed | tf_op | source)
XLA Modules:
  0.0 110.2 jit_solution(7617473931635792090)
XLA Ops:
  1.3 104.8 %shard_map.187 = (bf16[128,1536]{1,0:T(8,128)(2,1)}, bf16[128,1536]{1,0:T(8,128)(2,1)}, bf16[128,1536]{1,0:T(8,128)(2,1)}, bf16[128,1536]{1,0:T(8,128)(2,1)}, bf...) custom-call(s32[1]{0:T(128)S(6)} %copy.21.len_ref, bf16[128,1536]{1,0:T(8,128)(2,1)} %bitcast.16, ...), custom_call_target="tpu_custom_call" | custom-call | tf_op jit(solution)/shard_map/pallas_call | solution.py:787
  106.1 4.0 %shard_map.188 = (bf16[128,1536]{1,0:T(8,128)(2,1)}, bf16[128,1536]{1,0:T(8,128)(2,1)}, bf16[128,1536]{1,0:T(8,128)(2,1)}, bf16[128,1536]{1,0:T(8,128)(2,1)}, bf...) custom-call(f32[16,1664]{1,0:T(8,128)} %get-tuple-element.25.gw_ref,, ...), custom_call_target="tpu_custom_call" | custom-call | tf_op jit(solution)/shard_map/pallas_call | solution.py:820

commit v5 on v4

--- a/solution.py
+++ b/solution.py
@@ -37,16 +37,16 @@
     bo_hbm, gr_hbm, gq_hbm, gk_hbm, gv_hbm, gw_ref, gp_ref,
     q_ref, k_ref, v_ref, res_ref, go_ref, bo_ref, gr_ref, gq_ref, gk_ref, gv_ref, wo, wp, snd, rcv, kaug, qaug, vta, vaug, pt, inv, obuf, att_t, att, mixed, n1, r1, cin, cp, csum,
     gact, gm, act, gc, gcl, gpad, vacc, lh, rh, dsnd, do, doaug, qz, dz, kt, rq, rkv,
-    ng, cg, small_t, rows_t, rows_p, *rest,
+    ng, cg, small_t, rows_t, rows_p, rows_y, *rest,
 ):
     me = lax.axis_index("ctx")
     dp = lax.axis_index("dp")
     length = len_ref[0]
-    sums, rest = [rest[7 * i : 7 * i + 7] for i in range(4)], rest[28:]
+    sums, rest = [rest[7 * i : 7 * i + 7] for i in range(5)], rest[35:]
     (
-        wide, w_sem, i_sem, e_sem, s_q, r_q, s_o, r_o, s_d, r_d, s_g, r_g, s_k, r_k, s_h, r_h, s_r, r_r,
+        wide, flat, w_sem, i_sem, e_sem, s_q, r_q, s_o, r_o, s_d, r_d, s_g, r_g, s_k, r_k, s_h, r_h, s_r, r_r,
     ) = rest
-    dst = wp.at[pl.ds(0, S), pl.ds(0, S)]
+    dst = wo.at[pl.ds(0, S), pl.ds(0, S)]
     sq, skv = snd.at[:, :, pl.ds(0, HD)], snd.at[:, :, pl.ds(HD, 2 * HD)]
     core = lax.rem(dp, 2)
     y = lax.rem(lax.div(dp, 2), 2)
@@ -69,6 +69,12 @@
 
     def x_device(offset):
         return (dp, 4 * y_low + in_x(offset))
+
+    def in_y(offset):
+        return lax.rem(2 * y + y_low + (offset + 4), 4)
+
+    def side_device(offset):
+        return (4 * z + 2 * lax.div(in_y(offset), 2) + core, 4 * lax.rem(in_y(offset), 2) + x)
 
     def y_device(other, offset):
         return (dp + 2 - 4 * y if other else dp, at(offset))
@@ -184,13 +190,19 @@
         def cores(i):
             return to(term.at[1 - core, i], first.at[i], i, sibling)
 
-        def start():
-            order = (opposite, opposite + 1, up + 1, down, up, down + 1, 2 * here, 2 * here + 1)
-            for i, copy in zip(order, far_copies + plain_copies + (None,) * 4):
+        def begin(blocks, copies):
+            for i, copy in zip(blocks, copies):
                 cores(i).wait_recv()
                 term[core, i] = term[core, i] + first[i]
                 if copy is not None:
                     copy.start()
+
+        def start():
+            begin((opposite, opposite + 1), far_copies)
+
+        def more():
+            blocks = (up + 1, down, up, down + 1, 2 * here, 2 * here + 1)
+            begin(blocks, plain_copies + (None,) * 4)
 
         def join():
             for a, (copy, i) in enumerate(zip(far_copies, (up, down + 1))):
@@ -213,16 +225,31 @@
             for copy in far_copies + plain_copies + joint_copies:
                 copy.wait_send()
 
-        return to, cores, start, join, total, drain
-
-    def slices(part, split, count):
-        rows, width = part.shape
-        wide[rows : rows + 8, :width] = jnp.zeros((8, width), F32)
-        wide[:rows, :width] = part
+        return to, cores, (start, more), join, total, drain
+
+    def slices(part, split, count, width):
+        rows, full = part.shape
+        most = 3 * width // 4
+        wide[:rows, :full] = part
         for j in range(count):
-            split[j] = wide[12 * j : 12 * j + 16, :width].astype(BF)
-
-    def z_reducer(k):
+            flat[:12, :most] = wide[12 * j : 12 * j + 12, :most]
+            for g in range(3):
+                flat[12:, g * most // 3 : (g + 1) * most // 3] = wide[12 * j + 4 * g : 12 * j + 4 * g + 4, most:width]
+            if full > width:
+                flat[:12, most : most + full - width] = wide[12 * j : 12 * j + 12, width:full]
+            split[j] = flat[:, : most + full - width].astype(BF)
+
+    def unpacked(packed, target, begin, width):
+        most = 3 * width // 4
+        target[:12, begin : begin + most] = packed[:12, :most]
+        for g in range(3):
+            block = packed[12:, g * most // 3 : (g + 1) * most // 3]
+            target[4 * g : 4 * g + 4, begin + most : begin + width] = block
+        rest = packed.shape[1] - most
+        if rest:
+            target[:12, begin + width : begin + width + rest] = packed[:12, most:]
+
+    def z_reducer(k, width):
         to, cores, start, join, total, drain_ring = ring(k, in_z, z_device)
         split, last = sums[k][5], sums[k][6]
         others = [(b, o) for b in range(2) for o in range(N) if b or o]
@@ -237,7 +264,7 @@
 
         def spread():
             for a, part in enumerate(total()):
-                slices(part, split.at[a], N)
+                slices(part, split.at[a], N, width)
             for b, o in others:
                 sent(b, o).start()
             last[y, me] = split[y, me]
@@ -258,48 +285,45 @@
 
         return cores, start, join, spread, finish, drain
 
-    def x_reducer(k):
-        to, cores, start, join, total, drain_ring = ring(k, in_x, x_device)
+    def side_reducer(k, width, along, device, across, across_device):
+        to, cores, start, join, total, drain_ring = ring(k, along, device)
+        here, mine = along(0), across(0)
         term = sums[k][0]
         in_column, split, last = sums[k][4:]
 
         def column(o):
-            c = in_z(o)
+            c = across(o)
             rows = pl.ds(pl.multiple_of(48 * lax.rem(c, 2), 16), 48)
-            return to(term.at[core, 2 * x + lax.div(c, 2), rows], in_column.at[z], 13 + o, z_device(o))
+            block = term.at[core, 2 * here + lax.div(c, 2), rows]
+            return to(block, in_column.at[mine], 13 + o, across_device(o))
 
         def column_arrival(o):
-            block = in_column.at[in_z(-o)]
-            return to(block, block, 13 + o, z_device(-o))
-
-        def quad(b):
-            low, high = (1 - y_low if b // 2 else y_low), (1 - y if b % 2 else y)
-            return 2 * low + high, y_device(b % 2, 4 * (b // 2))
+            block = in_column.at[across(-o)]
+            return to(block, block, 13 + o, across_device(-o))
 
         def sent(b):
-            j, peer = quad(b)
-            return to(split.at[j], last.at[2 * y_low + y], 16 + b, peer)
+            return to(split.at[in_z(b)], last.at[z], 16 + b, z_device(b))
 
         def arrival(b):
-            j, peer = quad(b)
-            return to(last.at[j], last.at[j], 16 + b, peer)
-
-        def spread_z():
+            block = last.at[in_z(-b)]
+            return to(block, block, 16 + b, z_device(-b))
+
+        def spread_across():
             for a, part in enumerate(total()):
-                term[core, 2 * x + a] = part.astype(BF)
+                term[core, 2 * here + a] = part.astype(BF)
             for o in (1, 2, 3):
                 column(o).start()
 
         def spread():
-            own = pl.ds(pl.multiple_of(48 * lax.rem(z, 2), 16), 48)
-            part = term[core, 2 * x + lax.div(z, 2), own, :].astype(F32)
+            own = pl.ds(pl.multiple_of(48 * lax.rem(mine, 2), 16), 48)
+            part = term[core, 2 * here + lax.div(mine, 2), own, :].astype(F32)
             for o in (1, 2, 3):
                 column_arrival(o).wait_recv()
-                part = part + in_column[in_z(-o)].astype(F32)
-            slices(part, split, 4)
+                part = part + in_column[across(-o)].astype(F32)
+            slices(part, split, 4, width)
             for b in (1, 2, 3):
                 sent(b).start()
-            last[2 * y_low + y] = split[2 * y_low + y]
+            last[z] = split[z]
 
         def finish():
             for b in (1, 2, 3):
@@ -315,10 +339,12 @@
                 column(i).wait_send()
                 sent(i).wait_send()
 
-        return cores, start, join, spread, finish, drain, spread_z
-
-    point_z, point_x = z_reducer(0), x_reducer(1)
-    out_one, out_two = z_reducer(2), z_reducer(3)
+        return cores, start, join, spread, finish, drain, spread_across
+
+    point_z = z_reducer(0, 512)
+    point_x = side_reducer(1, 512, in_x, x_device, in_y, side_device)
+    point_y = side_reducer(2, 512, in_y, side_device, in_x, x_device)
+    out_one, out_two = z_reducer(3, 1024), z_reducer(4, 512)
 
     def weight_term(rows, others, begin, width, k, by_z, send):
         term = sums[k][0]
@@ -391,10 +417,13 @@
 
     def ordered(b, carry):
         r = iota((192, 1), 0)
-        d = 384 * lax.div(r, 48) + 48 * lax.rem(lax.div(r, 24), 2) + 192 * lax.rem(lax.div(r, 12), 2)
-        d = d + lax.rem(r, 12) + 96 * lax.div(b, 4) + 12 * lax.rem(b, 4)
-        pick = jnp.where(iota((192, D), 1) == d, 1.0, 0.0).astype(BF)
-        rows_p[pl.ds(pl.multiple_of(192 * b, 64), 192), :] = dot_nt(pick, gm[...]).astype(BF)
+        one, two = lax.div(r, 48), lax.rem(b, 4)
+        d = 384 * lax.rem(lax.div(r, 12), 4) + lax.rem(r, 12) + 96 * lax.div(b, 4)
+        by_x = 192 * lax.div(one, 2) + 48 * lax.rem(one, 2) + 12 * two
+        by_y = 192 * lax.div(two, 2) + 48 * lax.rem(two, 2) + 12 * one
+        for ref, more in ((rows_p, by_x), (rows_y, by_y)):
+            pick = jnp.where(iota((192, D), 1) == d + more, 1.0, 0.0).astype(BF)
+            ref[pl.ds(pl.multiple_of(192 * b, 64), 192), :] = dot_nt(pick, gm[...]).astype(BF)
         return carry
 
     lax.fori_loop(0, 8, ordered, 0)
@@ -404,6 +433,9 @@
     qz[HD:, :] = jnp.zeros((HD, S), BF)
     dz[:HD, :] = jnp.zeros((HD, S), BF)
     doaug[16:HD, :] = jnp.zeros((HD - 16, S), BF)
+
+    def turned(i):
+        return lax.rem(i + lax.div(me, 2) + 1, 4)
 
     for h in range(3):
         ex_q[h][1]()
@@ -420,6 +452,7 @@
             vaug[h, cols, :] = jnp.where(lane < HD, ones, both)
 
         def attend(i, carry, h=h):
+            i = turned(i)
             cols = pl.ds(pl.multiple_of(i * TILE, TILE), TILE)
             scores = dot(kaug[...], qaug[:, cols])
             top = jnp.max(scores, axis=0, keepdims=True)
@@ -459,8 +492,8 @@
     def mean_of(x):
         return jnp.sum(x, axis=1, keepdims=True) * (1.0 / D)
 
-    def first_norm(i, carry):
-        rows = pl.ds(pl.multiple_of(i * 16, 16), 16)
+    def first_norm(i):
+        rows = slice(i * 16, (i + 1) * 16)
         x = mixed[rows, :]
         x = x - mean_of(x)
         r = lax.rsqrt(mean_of(x * x) + EPSILON)
@@ -470,12 +503,9 @@
         valid = me * F + i * 16 + iota((16, 1), 0) < length
         low = jnp.where(valid, n * ng[...], 0.0).astype(BF)
         cin[rows, :] = low
-        wide = low.astype(F32)
+        low_wide = low.astype(F32)
         for c in range(NB):
-            cp[c, pl.ds(pl.multiple_of(16 + i * 16, 16), 16), :] = wide[:, c * 128 : (c + 1) * 128]
-        return carry
-
-    lax.fori_loop(0, F // 16, first_norm, 0)
+            cp[c, 16 + i * 16 : 32 + i * 16, :] = low_wide[:, c * 128 : (c + 1) * 128]
 
     def edges(buffer, k):
         to_right = pltpu.make_async_remote_copy(
@@ -503,22 +533,41 @@
             padded[c, 0:16, :] = left[:, c * 128 : (c + 1) * 128]
             padded[c, F + 16 : F + 32, :] = right[:, c * 128 : (c + 1) * 128]
 
+    ends = (0, F // 16 - 1)
+    for i in ends:
+        first_norm(i)
     halo = edges(cin, 0)
     for copy in halo:
         copy.start()
+    for i in range(1, F // 16 - 1):
+        first_norm(i)
+
+    def convolve(c, starts, count):
+        cols = pl.ds(pl.multiple_of(c * 128, 128), 128)
+        totals = [jnp.broadcast_to(cb_ref[pl.ds(c, 1), :], (count, 128))] * len(starts)
+        for t in range(KERN):
+            tap = taps_ref[t : t + 1, cols]
+            totals = [
+                total + cp[c, start + t + 1 : start + t + 1 + count, :] * tap
+                for total, start in zip(totals, starts)
+            ]
+        for total, start in zip(totals, starts):
+            csum[start : start + count, cols] = total
+
+    def convolve_inside(c, carry):
+        convolve(c, (16,), F - 32)
+        return carry
+
+    def convolve_ends(c, carry):
+        for a in range(2):
+            convolve(2 * c + a, (0, F - 16), 16)
+        return carry
+
+    lax.fori_loop(0, NB, convolve_inside, 0)
     for copy in halo:
         copy.wait()
     place_edges(0, cp)
-
-    def convolve(c, carry):
-        cols = pl.ds(pl.multiple_of(c * 128, 128), 128)
-        total = jnp.broadcast_to(cb_ref[pl.ds(c, 1), :], (F, 128))
-        for t in range(KERN):
-            total = total + cp[c, t + 1 : t + 1 + F, :] * taps_ref[t : t + 1, cols]
-        csum[:, cols] = total
-        return carry
-
-    lax.fori_loop(0, NB, convolve, 0)
+    lax.fori_loop(0, NB // 2, convolve_ends, 0)
 
     vacc[...] = jnp.zeros_like(vacc)
 
@@ -553,20 +602,14 @@
     for copy in halo2:
         copy.start()
 
-    weight_term(rows_t, act, 0, 768, 0, True, point_z[0])
-    weight_term(rows_p, act, 768, 768, 1, False, point_x[0])
-
-    def block_cols(c, carry):
-        cols = pl.ds(pl.multiple_of(c * 256, 256), 256)
-        bo_ref[:, cols] = (mixed[:, cols] + dot(act[...], wp[:, cols])).astype(BF)
-        return carry
-
-    lax.fori_loop(0, D // 256, block_cols, 0)
-    stores = [pltpu.make_async_copy(bo_ref, bo_hbm, e_sem.at[0])]
-    stores[0].start()
-
-    point_z[1]()
-    point_x[1]()
+    weight_term(rows_t, act, 0, 512, 0, True, point_z[0])
+    weight_term(rows_p, act, 512, 512, 1, False, point_x[0])
+    weight_term(rows_y, act, 1024, 512, 2, False, point_y[0])
+
+    points = (point_z, point_x, point_y)
+    for part in (0, 1):
+        for point in points:
+            point[1][part]()
 
     for copy in halo2:
         copy.wait()
@@ -593,8 +636,8 @@
         return carry
 
     lax.fori_loop(0, F // 16, first_norm_back, 0)
-    stores.append(pltpu.make_async_copy(gr_ref, gr_hbm, e_sem.at[1]))
-    stores[1].start()
+    stores = [pltpu.make_async_copy(gr_ref, gr_hbm, e_sem.at[1])]
+    stores[0].start()
 
     for h in range(3):
 
@@ -609,10 +652,12 @@
         lax.fori_loop(0, 2, attended_rows, 0)
         ex_d[h][0]()
 
+    turn(gr_ref)
+    weight_term(rows_t, att, 0, 1024, 3, True, out_one[0])
     point_z[2]()
     point_x[2]()
-    turn(gr_ref)
-    weight_term(rows_t, att, 0, 768, 2, True, out_one[0])
+    point_y[2]()
+    out_one[1][0]()
     small = csum
 
     def tap_rows(c, carry):
@@ -628,8 +673,12 @@
     small[KERN + 3 :, :] = jnp.zeros((128 - KERN - 3, D), F32)
     for c in range(NB):
         small_t[c * 128 : (c + 1) * 128, :] = small[:, c * 128 : (c + 1) * 128].T.astype(BF)
-    weight_term(rows_t, att, 768, 768, 3, True, out_two[0])
-    out_one[1]()
+    weight_term(rows_t, att, 1024, 512, 4, True, out_two[0])
+    out_two[1][0]()
+    out_one[1][1]()
+    out_two[1][1]()
+    point_x[6]()
+    point_y[6]()
     for h in range(3):
         ex_q[h][2]()
 
@@ -650,6 +699,7 @@
             kt[:, cols] = rcv[h, j, HD : 2 * HD, :]
 
         def back_queries(i, carry, h=h):
+            i = turned(i)
             cols = pl.ds(pl.multiple_of(i * TILE, TILE), TILE)
             grads = dot(vaug[h], doaug[:, cols])
             grads = (pt[h, :, cols].astype(F32) * grads).astype(BF)
@@ -664,6 +714,7 @@
         lax.fori_loop(0, S // TILE, back_queries, 0)
 
         def back_keys(j, carry, h=h):
+            j = at(j + 1)
             rows = pl.ds(pl.multiple_of(j * F, F), F)
             both = dot_nt(dst[rows, :], qz[...]) + dot_nt(pt[h, rows, :], dz[...])
             skv[h, j] = both.T.astype(BF)
@@ -675,14 +726,20 @@
         ex_k[h][4]()
         if h == 0:
             out_one[2]()
-            out_two[1]()
-            point_x[6]()
             point_z[3]()
         elif h == 1:
+            out_two[2]()
             point_x[3]()
-        else:
-            out_one[3]()
-            out_two[2]()
+            point_y[3]()
+
+    def block_cols(c, carry):
+        cols = pl.ds(pl.multiple_of(c * 256, 256), 256)
+        bo_ref[:, cols] = (mixed[:, cols] + dot(act[...], wp[:, cols])).astype(BF)
+        return carry
+
+    lax.fori_loop(0, D // 256, block_cols, 0)
+    stores.append(pltpu.make_async_copy(bo_ref, bo_hbm, e_sem.at[0]))
+    stores[-1].start()
 
     for h in range(3):
         ex_g[h][1]()
@@ -699,13 +756,18 @@
             stores.append(pltpu.make_async_copy(ref.at[:, cols], hbm.at[:, cols], e_sem.at[2 + 3 * h + a]))
             stores[-1].start()
         if h == 1:
+            out_one[3]()
+        elif h == 2:
             out_two[3]()
 
-    gp_ref[:, :768] = point_z[4]()
-    gp_ref[:, 768:] = point_x[4]()
-    gw_ref[:, :768] = out_one[4]()
-    gw_ref[:, 768:] = out_two[4]()
-    for reducer in (point_z, point_x, out_one, out_two):
+    gp_ref[12:, :] = jnp.zeros((4, D), F32)
+    gw_ref[12:, :] = jnp.zeros((4, D + 128), F32)
+    unpacked(point_z[4](), gp_ref, 0, 512)
+    unpacked(point_x[4](), gp_ref, 512, 512)
+    unpacked(point_y[4](), gp_ref, 1024, 512)
+    unpacked(out_one[4](), gw_ref, 0, 1024)
+    unpacked(out_two[4](), gw_ref, 1024, 512)
+    for reducer in (point_z, point_x, point_y, out_one, out_two):
         reducer[5]()
     for group in (ex_o, ex_d, ex_g, ex_k):
         for h in range(3):
@@ -763,16 +825,24 @@
         pltpu.VMEM((D, 128), BF),
         pltpu.VMEM((D, F), BF),
         pltpu.VMEM((D, F), BF),
+        pltpu.VMEM((D, F), BF),
         *[
-            pltpu.VMEM(shape + (width,), BF)
-            for width, by_z in ((768, True), (768, False), (768, True), (896, True))
+            pltpu.VMEM(shape, BF)
+            for w, last, by_z in (
+                (512, 384, True), (512, 384, False), (512, 384, False), (1024, 768, True), (640, 512, True)
+            )
             for shape in (
-                ((2, 8, 96), (8, 96), (2, 96), (2, 2, 96), (8,), (2, N, 16), (2, N, 16))
-                if by_z
-                else ((2, 8, 96), (8, 96), (2, 96), (2, 2, 96), (4, 48), (4, 16), (4, 16))
+                (2, 8, 96, w),
+                (8, 96, w),
+                (2, 96, w),
+                (2, 2, 96, w),
+                (8, w) if by_z else (4, 48, w),
+                (2, N, 16, last) if by_z else (4, 16, last),
+                (2, N, 16, last) if by_z else (4, 16, last),
             )
         ],
-        pltpu.VMEM((104, 896), F32),
+        pltpu.VMEM((96, 1024), F32),
+        pltpu.VMEM((16, 768), F32),
         dma((2,)),
         dma((5,)),
         dma((11,)),
@@ -782,7 +852,7 @@
         dma((3, N)), dma((3, N)),
         dma((3, N)), dma((3, N)),
         dma((4,)), dma((4,)),
-        dma((4, 30)), dma((4, 30)),
+        dma((5, 30)), dma((5, 30)),
     ]
     return pl.pallas_call(
         kernel,

time: 110 us -> 98.3 us (0.89); the launches traced: 110 us -> 97.3 us
  Pallas kernels: 109 us -> 95.8 us
    pallas_call x1, Pallas kernels: 105 us -> 91.9 us  [fused(): pl.pallas_call(kernel, out_shape=[rows] * 5 + [jax.ShapeDtypeStruct((16,...]
where the time goes in v5:
time: 98.3 us; the launch traced here: 97.3 us
  Pallas kernels  95.8 us (97%)
  between operations  1.46 us (1%)
    pallas_call x1, Pallas kernels, fused(): pl.pallas_call(kernel, out_shape=[rows] * 5 + [jax.ShapeDtypeStruct((16,...  91.9 us
    pallas_call x1, Pallas kernels, finished(): pl.pallas_call(finish, out_shape=[jax.ShapeDtypeStruct((F, D), BF)] * 5 +...  3.97 us

profile of v5, /device:TPU:0, one launch (start us, length us, event | category | flops | bytes accessed | tf_op | source)
XLA Modules:
  0.0 97.3 jit_solution(12397757967773506350)
XLA Ops:
  1.3 91.9 %shard_map.187 = (bf16[128,1536]{1,0:T(8,128)(2,1)}, bf16[128,1536]{1,0:T(8,128)(2,1)}, bf16[128,1536]{1,0:T(8,128)(2,1)}, bf16[128,1536]{1,0:T(8,128)(2,1)}, bf...) custom-call(s32[1]{0:T(128)S(6)} %copy.21.len_ref, bf16[128,1536]{1,0:T(8,128)(2,1)} %bitcast.16, ...), custom_call_target="tpu_custom_call" | custom-call | tf_op jit(solution)/shard_map/pallas_call | solution.py:857
  93.2 4.0 %shard_map.188 = (bf16[128,1536]{1,0:T(8,128)(2,1)}, bf16[128,1536]{1,0:T(8,128)(2,1)}, bf16[128,1536]{1,0:T(8,128)(2,1)}, bf16[128,1536]{1,0:T(8,128)(2,1)}, bf...) custom-call(f32[16,1664]{1,0:T(8,128)} %get-tuple-element.25.gw_ref,, ...), custom_call_target="tpu_custom_call" | custom-call | tf_op jit(solution)/shard_map/pallas_call | solution.py:890

commit v6 on v5

--- a/solution.py
+++ b/solution.py
@@ -33,18 +33,18 @@
 
 
 def kernel(
-    len_ref, q_hbm, k_hbm, v_hbm, res_hbm, go_hbm, wo_hbm, wp_hbm, ng_ref, taps_ref, cb_ref, cg_ref,
-    bo_hbm, gr_hbm, gq_hbm, gk_hbm, gv_hbm, gw_ref, gp_ref,
+    len_hbm, q_hbm, k_hbm, v_hbm, res_hbm, go_hbm, wo_hbm, wp_hbm, ng_hbm, taps_hbm, cb_hbm, cg_hbm,
+    bo_hbm, gr_hbm, gq_hbm, gk_hbm, gv_hbm, gw_hbm, gp_hbm,
+    len_ref, ng_ref, taps_ref, cb_ref, cg_ref, gw_ref, gp_ref,
     q_ref, k_ref, v_ref, res_ref, go_ref, bo_ref, gr_ref, gq_ref, gk_ref, gv_ref, wo, wp, snd, rcv, kaug, qaug, vta, vaug, pt, inv, obuf, att_t, att, mixed, n1, r1, cin, cp, csum,
     gact, gm, act, gc, gcl, gpad, vacc, lh, rh, dsnd, do, doaug, qz, dz, kt, rq, rkv,
     ng, cg, small_t, rows_t, rows_p, rows_y, *rest,
 ):
     me = lax.axis_index("ctx")
     dp = lax.axis_index("dp")
-    length = len_ref[0]
     sums, rest = [rest[7 * i : 7 * i + 7] for i in range(5)], rest[35:]
     (
-        wide, flat, w_sem, i_sem, e_sem, s_q, r_q, s_o, r_o, s_d, r_d, s_g, r_g, s_k, r_k, s_h, r_h, s_r, r_r,
+        wide, flat, w_sem, i_sem, e_sem, s_q, r_q, s_v, r_v, s_o, r_o, s_d, r_d, s_g, r_g, s_k, r_k, s_h, r_h, s_r, r_r,
     ) = rest
     dst = wo.at[pl.ds(0, S), pl.ds(0, S)]
     sq, skv = snd.at[:, :, pl.ds(0, HD)], snd.at[:, :, pl.ds(HD, 2 * HD)]
@@ -88,9 +88,10 @@
 
     loads = [
         pltpu.make_async_copy(source, target, i_sem.at[i])
-        for i, (source, target) in enumerate(
-            ((q_hbm, q_ref), (k_hbm, k_ref), (v_hbm, v_ref), (go_hbm, go_ref), (res_hbm, res_ref))
-        )
+        for i, (source, target) in enumerate((
+            (q_hbm, q_ref), (k_hbm, k_ref), (v_hbm, v_ref), (go_hbm, go_ref), (res_hbm, res_ref),
+            (len_hbm, len_ref), (ng_hbm, ng_ref), (taps_hbm, taps_ref), (cb_hbm, cb_ref), (cg_hbm, cg_ref),
+        ))
     ]
     for load in loads:
         load.start()
@@ -142,6 +143,11 @@
         def keep():
             target[h, me] = source[h, me]
 
+        def wait_one(j):
+            @pl.when(j != me)
+            def _():
+                arrival(lax.rem(me - j + N, N)).wait_recv()
+
         def wait():
             for o in range(1, N):
                 arrival(o).wait_recv()
@@ -150,9 +156,12 @@
             for o in range(1, N):
                 copy(o).wait_send()
 
-        return start, wait, drain, start_one, keep
-
-    ex_q = [exchange(snd, rcv, s_q, r_q, h) for h in range(3)]
+        return start, wait, drain, start_one, keep, wait_one
+
+    ex_q = [exchange(snd.at[:, :, pl.ds(0, HD)], rcv.at[:, :, pl.ds(0, HD)], s_q, r_q, h) for h in range(3)]
+    ex_v = [
+        exchange(snd.at[:, :, pl.ds(HD, 2 * HD)], rcv.at[:, :, pl.ds(HD, 2 * HD)], s_v, r_v, h) for h in range(3)
+    ]
     ex_o = [exchange(obuf, att_t, s_o, r_o, h) for h in range(3)]
     ex_d = [exchange(dsnd, do, s_d, r_d, h) for h in range(3)]
     ex_g = [exchange(sq, rq, s_g, r_g, h) for h in range(3)]
@@ -346,10 +355,11 @@
     point_y = side_reducer(2, 512, in_y, side_device, in_x, x_device)
     out_one, out_two = z_reducer(3, 1024), z_reducer(4, 512)
 
-    def weight_term(rows, others, begin, width, k, by_z, send):
+    def weight_term(rows, others, begin, width, k, by_z, along, send):
         term = sums[k][0]
 
         def block(i, carry):
+            i = lax.rem(i + 2 * along(2), 8) if by_z else lax.rem(i + along(2), 4)
             for a in range(2):
                 if by_z and a:
                     break
@@ -395,8 +405,12 @@
                 snd[h, 2 * b + 1, a * HD : (a + 1) * HD, :] = block[HD:]
         if h == 0:
             pl.semaphore_wait(barrier, len(peers))
+        ex_v[h][0]()
         ex_q[h][0]()
 
+    for load in loads[5:]:
+        load.wait()
+    length = len_ref[0]
     for c in range(NB):
         ng[:, c * 128 : (c + 1) * 128] = ng_ref[c : c + 1, :]
         cg[:, c * 128 : (c + 1) * 128] = cg_ref[c : c + 1, :]
@@ -438,11 +452,10 @@
         return lax.rem(i + lax.div(me, 2) + 1, 4)
 
     for h in range(3):
-        ex_q[h][1]()
+        ex_v[h][1]()
         lane = iota((F, 128), 1)
         for j in range(N):
             cols = slice(j * F, (j + 1) * F)
-            qaug[:HD, cols] = rcv[h, j, :HD, :]
             vta[:HD, cols] = rcv[h, j, 2 * HD :, :]
             both = rcv[h, j, HD:, :].T
             bias = jnp.where(j * F + iota((F, 128), 0) < length, 0.0, MASKED)
@@ -454,6 +467,10 @@
         def attend(i, carry, h=h):
             i = turned(i)
             cols = pl.ds(pl.multiple_of(i * TILE, TILE), TILE)
+            for a in range(TILE // F):
+                j = i * (TILE // F) + a
+                ex_q[h][5](j)
+                qaug[:HD, pl.ds(pl.multiple_of(j * F, F), F)] = rcv[h, j, :HD, :]
             scores = dot(kaug[...], qaug[:, cols])
             top = jnp.max(scores, axis=0, keepdims=True)
             weights = jnp.exp(scores - top).astype(BF)
@@ -602,9 +619,9 @@
     for copy in halo2:
         copy.start()
 
-    weight_term(rows_t, act, 0, 512, 0, True, point_z[0])
-    weight_term(rows_p, act, 512, 512, 1, False, point_x[0])
-    weight_term(rows_y, act, 1024, 512, 2, False, point_y[0])
+    weight_term(rows_t, act, 0, 512, 0, True, in_z, point_z[0])
+    weight_term(rows_p, act, 512, 512, 1, False, in_x, point_x[0])
+    weight_term(rows_y, act, 1024, 512, 2, False, in_y, point_y[0])
 
     points = (point_z, point_x, point_y)
     for part in (0, 1):
@@ -625,17 +642,17 @@
 
     lax.fori_loop(0, NB, convolve_back, 0)
 
-    def first_norm_back(i, carry):
-        rows = pl.ds(pl.multiple_of(i * 16, 16), 16)
+    def first_norm_back(i):
+        rows = slice(i * 16, (i + 1) * 16)
         x = csum[rows, :]
         n = n1[rows, :]
         vacc[1] += fold(x * n)
         u = x * ng[...]
         grad = r1[rows, :] * (u - mean_of(u) - n * mean_of(u * n))
         gr_ref[rows, :] = (gm[rows, :].astype(F32) + grad).astype(BF)
-        return carry
-
-    lax.fori_loop(0, F // 16, first_norm_back, 0)
+
+    for i in range(F // 16):
+        first_norm_back(i)
     stores = [pltpu.make_async_copy(gr_ref, gr_hbm, e_sem.at[1])]
     stores[0].start()
 
@@ -653,7 +670,7 @@
         ex_d[h][0]()
 
     turn(gr_ref)
-    weight_term(rows_t, att, 0, 1024, 3, True, out_one[0])
+    weight_term(rows_t, att, 0, 1024, 3, True, in_z, out_one[0])
     point_z[2]()
     point_x[2]()
     point_y[2]()
@@ -673,7 +690,7 @@
     small[KERN + 3 :, :] = jnp.zeros((128 - KERN - 3, D), F32)
     for c in range(NB):
         small_t[c * 128 : (c + 1) * 128, :] = small[:, c * 128 : (c + 1) * 128].T.astype(BF)
-    weight_term(rows_t, att, 1024, 512, 4, True, out_two[0])
+    weight_term(rows_t, att, 1024, 512, 4, True, in_z, out_two[0])
     out_two[1][0]()
     out_one[1][1]()
     out_two[1][1]()
@@ -681,6 +698,7 @@
     point_y[6]()
     for h in range(3):
         ex_q[h][2]()
+        ex_v[h][2]()
 
     for h in range(3):
         ex_d[h][1]()
@@ -767,6 +785,9 @@
     unpacked(point_y[4](), gp_ref, 1024, 512)
     unpacked(out_one[4](), gw_ref, 0, 1024)
     unpacked(out_two[4](), gw_ref, 1024, 512)
+    for i, (ref, hbm) in enumerate(((gw_ref, gw_hbm), (gp_ref, gp_hbm))):
+        stores.append(pltpu.make_async_copy(ref, hbm, e_sem.at[11 + i]))
+        stores[-1].start()
     for reducer in (point_z, point_x, point_y, out_one, out_two):
         reducer[5]()
     for group in (ex_o, ex_d, ex_g, ex_k):
@@ -777,12 +798,17 @@
 
 
 def fused(lengths, q, k, v, res, go, wo, wp, ng, taps, cb, cg):
-    vmem = pl.BlockSpec(memory_space=pltpu.VMEM)
     hbm = pl.BlockSpec(memory_space=pl.ANY)
-    smem = pl.BlockSpec(memory_space=pltpu.SMEM)
     rows = jax.ShapeDtypeStruct((F, D), BF)
     dma = pltpu.SemaphoreType.DMA
     scratch = [
+        pltpu.SMEM((1,), jnp.int32),
+        pltpu.VMEM((NB, 128), F32),
+        pltpu.VMEM((KERN, D), F32),
+        pltpu.VMEM((NB, 128), F32),
+        pltpu.VMEM((NB, 128), F32),
+        pltpu.VMEM((16, D + 128), F32),
+        pltpu.VMEM((16, D), F32),
         *[pltpu.VMEM((F, D), BF)] * 10,
         pltpu.VMEM((D, D), BF),
         pltpu.VMEM((D, D), BF),
@@ -844,8 +870,9 @@
         pltpu.VMEM((96, 1024), F32),
         pltpu.VMEM((16, 768), F32),
         dma((2,)),
-        dma((5,)),
-        dma((11,)),
+        dma((10,)),
+        dma((13,)),
+        dma((3, N)), dma((3, N)),
         dma((3, N)), dma((3, N)),
         dma((3, N)), dma((3, N)),
         dma((3, N)), dma((3, N)),
@@ -858,8 +885,8 @@
         kernel,
         out_shape=[rows] * 5
         + [jax.ShapeDtypeStruct((16, D + 128), F32), jax.ShapeDtypeStruct((16, D), F32)],
-        in_specs=[smem] + [hbm] * 7 + [vmem] * 4,
-        out_specs=[hbm] * 5 + [vmem] * 2,
+        in_specs=[hbm] * 12,
+        out_specs=[hbm] * 7,
         scratch_shapes=scratch,
         compiler_params=pltpu.CompilerParams(
             collective_id=0, has_side_effects=True, vmem_limit_bytes=62 * 1024 * 1024
@@ -867,35 +894,44 @@
     )(lengths, q, k, v, res, go, wo, wp, ng, taps, cb, cg)
 
 
-def finish(gw_ref, gp_ref, *refs):
-    sources, targets, (gow_ref, gpw_ref, gker_ref, gvec_ref), (held, sems) = refs[:5], refs[5:10], refs[10:14], refs[14:]
-    inward = [pltpu.make_async_copy(sources[i], held.at[i], sems.at[0, i]) for i in range(5)]
-    outward = [pltpu.make_async_copy(held.at[i], targets[i], sems.at[1, i]) for i in range(5)]
+def finish(*refs):
+    sources, targets, held, results, sems = refs[:7], refs[7:16], refs[16:23], refs[23:27], refs[27]
+    inward = [pltpu.make_async_copy(sources[i], held[i], sems.at[0, i]) for i in range(7)]
+    outward = [pltpu.make_async_copy(held[i], targets[i], sems.at[1, i]) for i in range(5)]
+    outward += [pltpu.make_async_copy(results[i], targets[5 + i], sems.at[1, 5 + i]) for i in range(4)]
     for copy in inward:
         copy.start()
     for i in range(5):
         inward[i].wait()
         outward[i].start()
-    gow_ref[...] = gw_ref[:12, :D]
-    gpw_ref[...] = gp_ref[:12, :]
-    gker_ref[...] = gw_ref[:12, D : D + KERN]
-    gvec_ref[...] = gw_ref[:, D:].T[KERN : KERN + 3, :12]
+    inward[5].wait()
+    inward[6].wait()
+    gw_ref, gp_ref = held[5:]
+    results[0][...] = gw_ref[:12, :D]
+    results[1][...] = gp_ref[:12, :]
+    results[2][...] = gw_ref[:12, D : D + KERN]
+    results[3][...] = gw_ref[:, D:].T[KERN : KERN + 3, :12]
+    for copy in outward[5:]:
+        copy.start()
     for copy in outward:
         copy.wait()
 
 
 def finished(rows, gw, gp):
-    vmem = pl.BlockSpec(memory_space=pltpu.VMEM)
     hbm = pl.BlockSpec(memory_space=pl.ANY)
+    shapes = ((12, D), (12, D), (12, KERN), (3, 12))
     return pl.pallas_call(
         finish,
-        out_shape=[jax.ShapeDtypeStruct((F, D), BF)] * 5
-        + [jax.ShapeDtypeStruct(shape, F32) for shape in ((12, D), (12, D), (12, KERN), (3, 12))],
-        in_specs=[vmem] * 2 + [hbm] * 5,
-        out_specs=[hbm] * 5 + [vmem] * 4,
-        scratch_shapes=[pltpu.VMEM((5, F, D), BF), pltpu.SemaphoreType.DMA((2, 5))],
+        out_shape=[jax.ShapeDtypeStruct((F, D), BF)] * 5 + [jax.ShapeDtypeStruct(shape, F32) for shape in shapes],
+        in_specs=[hbm] * 7,
+        out_specs=[hbm] * 9,
+        scratch_shapes=[
+            *[pltpu.VMEM((F, D), BF)] * 5,
+            *[pltpu.VMEM(shape, F32) for shape in ((16, D + 128), (16, D), *shapes)],
+            pltpu.SemaphoreType.DMA((2, 9)),
+        ],
         compiler_params=pltpu.CompilerParams(vmem_limit_bytes=62 * 1024 * 1024),
-    )(gw, gp, *rows)
+    )(*rows, gw, gp)
 
 
 def local(

time: 98.3 us -> 94.1 us (0.957)
  Pallas kernels: 95.8 us -> 91.8 us
    pallas_call x1, Pallas kernels: 91.9 us -> 89.3 us  [fused(): pl.pallas_call(kernel, out_shape=[rows] * 5 + [jax.ShapeDtypeStruct((16,...]
    pallas_call x1, Pallas kernels: 3.97 us -> 2.48 us  [finished(): pl.pallas_call(finish, out_shape=[jax.ShapeDtypeStruct((F, D), BF)] * 5 +...]
where the time goes in v6:
time: 94.1 us; the launch traced here: 93.3 us
  Pallas kernels  91.8 us (98%)
  between operations  1.46 us (2%)
    pallas_call x1, Pallas kernels, fused(): pl.pallas_call(kernel, out_shape=[rows] * 5 + [jax.ShapeDtypeStruct((16,...  89.3 us
    pallas_call x1, Pallas kernels, finished(): pl.pallas_call(finish, out_shape=[jax.ShapeDtypeStruct((F, D), BF)] * 5 +...  2.48 us

profile of v6, /device:TPU:0, one launch (start us, length us, event | category | flops | bytes accessed | tf_op | source)
XLA Modules:
  0.0 93.3 jit_solution(6968423634792225663)
XLA Ops:
  1.3 89.3 %shard_map.187 = (bf16[128,1536]{1,0:T(8,128)(2,1)}, bf16[128,1536]{1,0:T(8,128)(2,1)}, bf16[128,1536]{1,0:T(8,128)(2,1)}, bf16[128,1536]{1,0:T(8,128)(2,1)}, bf...) custom-call(s32[1]{0:T(128)S(6)} %copy.21.len_hbm, bf16[128,1536]{1,0:T(8,128)(2,1)} %bitcast.16, ...), custom_call_target="tpu_custom_call" | custom-call | tf_op jit(solution)/shard_map/pallas_call | solution.py:884
  90.6 2.5 %shard_map.188 = (bf16[128,1536]{1,0:T(8,128)(2,1)}, bf16[128,1536]{1,0:T(8,128)(2,1)}, bf16[128,1536]{1,0:T(8,128)(2,1)}, bf16[128,1536]{1,0:T(8,128)(2,1)}, bf...) custom-call(bf16[128,1536]{1,0:T(8,128)(2,1)} %get-tuple-element.25., ...), custom_call_target="tpu_custom_call" | custom-call | tf_op jit(solution)/shard_map/pallas_call | solution.py:923

commit v7 on v6

--- a/solution.py
+++ b/solution.py
@@ -12,7 +12,7 @@
 HD = 64
 KERN = 31
 NB = D // 128
-TILE = 256
+TILE = 512
 EPSILON = 1e-05
 MASKED = -1e30
 MESH = pl.DeviceIdType.MESH
@@ -449,7 +449,7 @@
     doaug[16:HD, :] = jnp.zeros((HD - 16, S), BF)
 
     def turned(i):
-        return lax.rem(i + lax.div(me, 2) + 1, 4)
+        return lax.rem(i + lax.div(me, TILE // F) + 1, S // TILE)
 
     for h in range(3):
         ex_v[h][1]()
@@ -669,11 +669,11 @@
         lax.fori_loop(0, 2, attended_rows, 0)
         ex_d[h][0]()
 
-    turn(gr_ref)
-    weight_term(rows_t, att, 0, 1024, 3, True, in_z, out_one[0])
     point_z[2]()
     point_x[2]()
     point_y[2]()
+    turn(gr_ref)
+    weight_term(rows_t, att, 0, 1024, 3, True, in_z, out_one[0])
     out_one[1][0]()
     small = csum
 
@@ -732,14 +732,15 @@
         lax.fori_loop(0, S // TILE, back_queries, 0)
 
         def back_keys(j, carry, h=h):
-            j = at(j + 1)
-            rows = pl.ds(pl.multiple_of(j * F, F), F)
+            j = lax.rem(j + lax.div(me, 2) + 1, 4)
+            rows = pl.ds(pl.multiple_of(j * 2 * F, 2 * F), 2 * F)
             both = dot_nt(dst[rows, :], qz[...]) + dot_nt(pt[h, rows, :], dz[...])
-            skv[h, j] = both.T.astype(BF)
-            ex_k[h][3](j)
+            for a in range(2):
+                skv[h, 2 * j + a] = both[a * F : (a + 1) * F].T.astype(BF)
+                ex_k[h][3](2 * j + a)
             return carry
 
-        lax.fori_loop(0, N, back_keys, 0)
+        lax.fori_loop(0, N // 2, back_keys, 0)
         ex_g[h][4]()
         ex_k[h][4]()
         if h == 0:

time: 94.1 us -> 92.5 us (0.983)
  Pallas kernels: 91.8 us -> 90 us
    pallas_call x1, Pallas kernels: 89.3 us -> 87.5 us  [fused(): pl.pallas_call(kernel, out_shape=[rows] * 5 + [jax.ShapeDtypeStruct((16,...]
where the time goes in v7:
time: 92.5 us; the launch traced here: 91.5 us
  Pallas kernels  90 us (97%)
  between operations  1.46 us (2%)
    pallas_call x1, Pallas kernels, fused(): pl.pallas_call(kernel, out_shape=[rows] * 5 + [jax.ShapeDtypeStruct((16,...  87.5 us
    pallas_call x1, Pallas kernels, finished(): pl.pallas_call(finish, out_shape=[jax.ShapeDtypeStruct((F, D), BF)] * 5 +...  2.48 us

profile of v7, /device:TPU:0, one launch (start us, length us, event | category | flops | bytes accessed | tf_op | source)
XLA Modules:
  0.0 91.5 jit_solution(10175744207604642612)
XLA Ops:
  1.3 87.5 %shard_map.187 = (bf16[128,1536]{1,0:T(8,128)(2,1)}, bf16[128,1536]{1,0:T(8,128)(2,1)}, bf16[128,1536]{1,0:T(8,128)(2,1)}, bf16[128,1536]{1,0:T(8,128)(2,1)}, bf...) custom-call(s32[1]{0:T(128)S(6)} %copy.21.len_hbm, bf16[128,1536]{1,0:T(8,128)(2,1)} %bitcast.16, ...), custom_call_target="tpu_custom_call" | custom-call | tf_op jit(solution)/shard_map/pallas_call | solution.py:885
  88.8 2.5 %shard_map.188 = (bf16[128,1536]{1,0:T(8,128)(2,1)}, bf16[128,1536]{1,0:T(8,128)(2,1)}, bf16[128,1536]{1,0:T(8,128)(2,1)}, bf16[128,1536]{1,0:T(8,128)(2,1)}, bf...) custom-call(bf16[128,1536]{1,0:T(8,128)(2,1)} %get-tuple-element.25., ...), custom_call_target="tpu_custom_call" | custom-call | tf_op jit(solution)/shard_map/pallas_call | solution.py:924

commit v8 on v7

--- a/solution.py
+++ b/solution.py
@@ -774,9 +774,9 @@
         for a, (ref, hbm) in enumerate(((gq_ref, gq_hbm), (gk_ref, gk_hbm), (gv_ref, gv_hbm))):
             stores.append(pltpu.make_async_copy(ref.at[:, cols], hbm.at[:, cols], e_sem.at[2 + 3 * h + a]))
             stores[-1].start()
-        if h == 1:
+        if h == 0:
             out_one[3]()
-        elif h == 2:
+        elif h == 1:
             out_two[3]()
 
     gp_ref[12:, :] = jnp.zeros((4, D), F32)

time: 92.5 us -> 91.9 us (level)
  no operation moved by 1% of the time
where the time goes in v8:
time: 91.9 us; the launch traced here: 91.2 us
  Pallas kernels  89.7 us (98%)
  between operations  1.46 us (2%)
    pallas_call x1, Pallas kernels, fused(): pl.pallas_call(kernel, out_shape=[rows] * 5 + [jax.ShapeDtypeStruct((16,...  87.3 us
    pallas_call x1, Pallas kernels, finished(): pl.pallas_call(finish, out_shape=[jax.ShapeDtypeStruct((F, D), BF)] * 5 +...  2.48 us

profile of v8, /device:TPU:0, one launch (start us, length us, event | category | flops | bytes accessed | tf_op | source)
XLA Modules:
  0.0 91.2 jit_solution(12861226505972706212)
XLA Ops:
  1.3 87.3 %shard_map.187 = (bf16[128,1536]{1,0:T(8,128)(2,1)}, bf16[128,1536]{1,0:T(8,128)(2,1)}, bf16[128,1536]{1,0:T(8,128)(2,1)}, bf16[128,1536]{1,0:T(8,128)(2,1)}, bf...) custom-call(s32[1]{0:T(128)S(6)} %copy.21.len_hbm, bf16[128,1536]{1,0:T(8,128)(2,1)} %bitcast.16, ...), custom_call_target="tpu_custom_call" | custom-call | tf_op jit(solution)/shard_map/pallas_call | solution.py:885
  88.6 2.5 %shard_map.188 = (bf16[128,1536]{1,0:T(8,128)(2,1)}, bf16[128,1536]{1,0:T(8,128)(2,1)}, bf16[128,1536]{1,0:T(8,128)(2,1)}, bf16[128,1536]{1,0:T(8,128)(2,1)}, bf...) custom-call(bf16[128,1536]{1,0:T(8,128)(2,1)} %get-tuple-element.25., ...), custom_call_target="tpu_custom_call" | custom-call | tf_op jit(solution)/shard_map/pallas_call | solution.py:924
